TPU v7x, 256 devices: a whole 4x4x8 slice. The times are simulated.
256 devices in a mesh: dp: 4 (over z_lo, core), code: 64 (over x, y, z_hi).
Axes of the slice: x: 4, y: 4, z: 8 (z_hi: 4, z_lo: 2; z = z_hi * 2 + z_lo), core: 2. Of those that a mesh axis runs over, the one named last changes fastest.
Arguments:
- latents: bfloat16 [4096, 256], P(('dp', 'code')), may hold values from -32 to 32
- upstream: bfloat16 [4096, 256], P(('dp', 'code')), may hold values from -6 to 6
- targets: int32 [4096], P(('dp', 'code')), may hold values from 0 to 262143
- codebook: float32 [262144, 256], P('code'), may hold values from -1 to 1
- moment_one: float32 [64, 4096, 256], P('code', 'dp'), may hold values from -4 to 4
- moment_two: float32 [64, 4096, 256], P('code', 'dp'), may hold values from 0.01 to 1
Outputs:
- quantized: bfloat16 [4096, 256], P(('dp', 'code'))
- latent_grad: float32 [4096, 256], P(('dp', 'code'))
- new_codebook: float32 [64, 4096, 256], P('code', 'dp')
- new_moment_one: float32 [64, 4096, 256], P('code', 'dp')
- new_moment_two: float32 [64, 4096, 256], P('code', 'dp')
All inputs are finite; a program needn't handle non-finite values.
Results may differ from a plain program's by a relative error of at most 0.004.
Values may be sent and summed in bfloat16 or wider, within the bound.
A program may use at most 64 MiB of HBM per device.

v0:
```python
import jax
import jax.numpy as jnp
from jax import lax
from jax.sharding import PartitionSpec as P

ADAM_STEP = 100


logit_scale = 4.0
commit_weight = 0.5
learn_rate = 0.001
beta_one = 0.9
beta_two = 0.999
adam_eps = 1e-08


def combined_all(shard, axis, combine):
    everything = jax.tree.map(lambda part: lax.all_gather(part, axis), shard)
    initial = jax.tree.map(lambda part: part[0], everything)

    def lap(k, so_far):
        return combine(so_far, jax.tree.map(lambda part: part[k], everything))

    return lax.fori_loop(1, lax.axis_size(axis), lap, initial)


def score_pair(stacked, code_block, row_count):
    joined = lax.dot_general(
        stacked, code_block, (((1,), (1,)), ((), ())), preferred_element_type=jnp.float32
    )
    return (logit_scale * joined[:row_count], joined[row_count:])


def join_stats(earlier, later):
    peak_row = jnp.maximum(earlier[0], later[0])
    fade_early = jnp.exp(earlier[0] - peak_row)
    fade_late = jnp.exp(later[0] - peak_row)
    return (
        peak_row,
        earlier[1] * fade_early + later[1] * fade_late,
        earlier[2] * fade_early + later[2] * fade_late,
    )


def per_device(latents, upstream, targets, codebook, moment_one, moment_two):
    latent_all, upstream_all, target_all = (
        lax.all_gather(latents, "code", axis=0, tiled=True),
        lax.all_gather(upstream, "code", axis=0, tiled=True),
        lax.all_gather(targets, "code", axis=0, tiled=True),
    )
    row_count = latent_all.shape[0]
    shard_codes, channels = codebook.shape
    block_width = min(1024, shard_codes)
    codes_bf = codebook.astype(jnp.bfloat16)
    blocks = codes_bf.reshape(shard_codes // block_width, block_width, channels)
    stacked = jnp.concatenate([latent_all, upstream_all], axis=0)
    zeros_row = jnp.zeros((row_count,), jnp.float32)
    lowest = jnp.full((row_count,), -jnp.inf, jnp.float32)

    def scan_online(carry, code_block):
        scores, affinity = score_pair(stacked, code_block, row_count)
        peak_new = jnp.maximum(carry[0], jnp.max(scores, axis=1))
        fade_factor = jnp.exp(carry[0] - peak_new)
        exp_terms = jnp.exp(scores - peak_new[:, None])
        return (
            (
                peak_new,
                carry[1] * fade_factor + jnp.sum(exp_terms, axis=1),
                carry[2] * fade_factor + jnp.sum(exp_terms * affinity, axis=1),
            ),
            None,
        )

    (local_peak, local_mass, local_weighted), unused = lax.scan(
        scan_online, (lowest, zeros_row, zeros_row), blocks
    )
    row_max, total_mass, weighted = combined_all(
        (local_peak, local_mass, local_weighted), "code", join_stats
    )
    mean_affinity = weighted / total_mass

    def scan_grad(soft_grad, code_block):
        scores, affinity = score_pair(stacked, code_block, row_count)
        probability = jnp.exp(scores - row_max[:, None]) / total_mass[:, None]
        weights = (logit_scale * probability * (affinity - mean_affinity[:, None])).astype(
            jnp.bfloat16
        )
        soft_grad = soft_grad + jnp.dot(weights, code_block, preferred_element_type=jnp.float32)
        spread = lax.dot_general(
            weights, latent_all, (((0,), (0,)), ((), ())), preferred_element_type=jnp.float32
        )
        return (soft_grad, spread)

    soft_grad, spread_blocks = lax.scan(
        scan_grad, jnp.zeros((row_count, channels), jnp.float32), blocks
    )
    spread_all = spread_blocks.reshape(shard_codes, channels)
    shard_index = lax.axis_index("code")
    local_index = target_all - shard_index * shard_codes
    in_shard = (local_index >= 0) & (local_index < shard_codes)
    slot_index = jnp.where(in_shard, local_index, 0)
    lookup = jnp.where(in_shard[:, None], codebook[slot_index], 0.0)
    masked = jnp.where(in_shard[:, None], upstream_all.astype(jnp.float32), 0.0)
    picked = jax.ops.segment_sum(masked, slot_index, num_segments=shard_codes)
    grad_partial = spread_all + picked
    soft_own, quant_own = (
        lax.psum_scatter(soft_grad, "code", scatter_dimension=0, tiled=True),
        lax.psum_scatter(lookup, "code", scatter_dimension=0, tiled=True),
    )
    quantized = quant_own.astype(jnp.bfloat16)
    latent_grad = soft_own + commit_weight * (latents.astype(jnp.float32) - quant_own)
    quarter = shard_codes // lax.axis_size("dp")
    dp_index = lax.axis_index("dp")
    grad_total = lax.psum(grad_partial.astype(jnp.bfloat16), "dp").astype(jnp.float32)
    code_grad = lax.dynamic_slice_in_dim(grad_total, dp_index * quarter, quarter, 0)
    own_codes = lax.dynamic_slice_in_dim(codebook, dp_index * quarter, quarter, 0)
    fresh_one = beta_one * moment_one[0] + (1.0 - beta_one) * code_grad
    fresh_two = beta_two * moment_two[0] + (1.0 - beta_two) * code_grad * code_grad
    fix_one = 1.0 - beta_one**ADAM_STEP
    fix_two = 1.0 - beta_two**ADAM_STEP
    updated = own_codes - learn_rate * (fresh_one / fix_one) / (
        jnp.sqrt(fresh_two / fix_two) + adam_eps
    )
    return (quantized, latent_grad, updated[None], fresh_one[None], fresh_two[None])


def solution(mesh):
    return jax.shard_map(
        per_device,
        mesh=mesh,
        in_specs=(
            P(("dp", "code"), None),
            P(("dp", "code"), None),
            P(("dp", "code")),
            P("code", None),
            P("code", "dp", None),
            P("code", "dp", None),
        ),
        out_specs=(
            P(("dp", "code"), None),
            P(("dp", "code"), None),
            P("code", "dp", None),
            P("code", "dp", None),
            P("code", "dp", None),
        ),
        check_vma=False,
    )
```

profile of v0, /device:TPU:2, one launch (start us, length us, event | category | flops | bytes accessed | tf_op | source)
XLA Modules:
  0.0 1780.9 jit_solution(8671303637957741267)
XLA Ops:
  8.1 176.0 %all_gather.28 = bf16[1024,256]{1,0:T(8,128)(2,1)S(1)} all-gather(bf16[16,256]{1,0:T(8,128)(2,1)} %param.12), channel_id=1, replica_groups=mesh['dp'=4,'code'=64] {'code'}, dimensions={0}, use_global_device_ids=true | all-gather | bytes 532480 | tf_op jit(solution)/shard_map/all_gather | solution.py:47
  184.9 172.2 %all_gather.29 = bf16[1024,256]{1,0:T(8,128)(2,1)S(1)} all-gather(bf16[16,256]{1,0:T(8,128)(2,1)} %param.13), channel_id=1, replica_groups=mesh['dp'=4,'code'=64] {'code'}, dimensions={0}, use_global_device_ids=true | all-gather | bytes 532480 | tf_op jit(solution)/shard_map/all_gather | solution.py:48
  357.1 3.9 convert_element_type.22
  361.1 42.0 %while.48 = (s32[]{:T(128)}, f32[1024]{0:T(1024)S(1)}, f32[1024]{0:T(1024)S(1)}, f32[1024]{0:T(1024)S(1)}, bf16[4,1024,256]{2,1,0:T(8,128)(2,1)}, /*index=5*/bf16[2048,256]{1,0:T(8,128)(2,1)S(1)}, s32[]{:T(128)}, s32[]{:T(128)}) while((s32[]{:T(128)}, f32[1024]{0:T(1024)S(1)}, f32[1024]{0:T(1024)S(1)}, f32[1024]{0:T(1024)S(1)}, ...), condition=%wide.region_5.6_spmd.clone, body=%wide.region_1.5_spmd.clone.sunk | while | flops 1081089024 | bytes 56169080 | solution.py:74
  361.1 2.3 convolution_bitcast_fusion.5
  363.4 3.2 copy-done
  367.0 4.5 fusion.52
  371.6 2.3 convolution_bitcast_fusion.5
  373.9 3.2 copy-done
  377.5 4.5 fusion.52
  382.1 2.3 convolution_bitcast_fusion.5
  384.4 3.2 copy-done
  388.0 4.5 fusion.52
  394.9 3.2 copy-done
  398.5 4.5 fusion.52
  403.1 187.7 %all-gather = f32[65536]{0:T(1024)S(1)} all-gather(f32[1024]{0:T(1024)S(1)} %get-tuple-element.265), channel_id=2, replica_groups=mesh['dp'=4,'code'=64] {'code'}, dimensions={0}, use_global_device_ids=true | all-gather | bytes 266240 | tf_op jit(solution)/shard_map/all_gather | solution.py:18
  590.8 185.0 %all-gather.1 = f32[65536]{0:T(1024)S(1)} all-gather(f32[1024]{0:T(1024)S(1)} %get-tuple-element.266), channel_id=3, replica_groups=mesh['dp'=4,'code'=64] {'code'}, dimensions={0}, use_global_device_ids=true | all-gather | bytes 266240 | tf_op jit(solution)/shard_map/all_gather | solution.py:18
  775.9 187.7 %all-gather.2 = f32[65536]{0:T(1024)S(1)} all-gather(f32[1024]{0:T(1024)S(1)} %get-tuple-element.267), channel_id=4, replica_groups=mesh['dp'=4,'code'=64] {'code'}, dimensions={0}, use_global_device_ids=true | all-gather | bytes 266240 | tf_op jit(solution)/shard_map/all_gather | solution.py:18
  963.7 6.9 while.47
  970.7 33.7 %while.49 = (s32[]{:T(128)}, f32[1024,256]{1,0:T(8,128)}, f32[4,1024,256]{2,1,0:T(8,128)}, bf16[4,1024,256]{2,1,0:T(8,128)(2,1)}, bf16[2048,256]{1,0:T(8,128)(2,...) while((s32[]{:T(128)}, f32[1024,256]{1,0:T(8,128)}, ...), condition=%wide.region_9.10_spmd.clone, body=%wide.region_8.9_spmd.clone.sunk | while | flops 2155347968 | bytes 30946960 | solution.py:94
  970.7 2.3 convolution_bitcast_fusion.6
  974.3 2.8 convolution_add_fusion.2
  982.5 3.2 convolution_add_fusion.2
  991.0 3.2 convolution_add_fusion.2
  999.5 3.2 convolution_add_fusion.2
  1006.0 49.4 %all-reduce = s32[1024]{0:T(1024)S(1)} all-reduce(s32[1024]{0:T(1024)S(1)} %dynamic-update-slice), channel_id=1, replica_groups=mesh['dp'=4,'code'=64] {'code'}, use_global_device_ids=true, to_apply=%add | all-reduce | flops 1024 | bytes 8192
  1055.4 5.7 gather_fusion
  1062.4 12.2 scatter_custom_fusion
  1074.6 3.9 convert_element_type.25
  1078.5 308.1 %reduce-scatter.5.cloned.1.call-done = f32[16,256]{1,0:T(8,128)} async-done(((f32[1024,256]{1,0:T(8,128)}), f32[16,256]{1,0:T(8,128)}) %reduce-scatter.5.cloned.1.call-update) | async-done | bytes 16400 | tf_op jit(solution)/shard_map/reduce_scatter | solution.py:107
  1386.6 381.6 %reduce-scatter.3.cloned.1.call-done = f32[16,256]{1,0:T(8,128)} async-done(((f32[1024,256]{1,0:T(8,128)}), f32[16,256]{1,0:T(8,128)}) %reduce-scatter.3.cloned.1.call-update) | async-done | bytes 16400 | tf_op jit(solution)/shard_map/reduce_scatter | solution.py:108
  1769.7 3.8 fusion.27
  (399 shorter events, 30.8 us)
Async XLA Ops:
  8.0 1378.6 %reduce-scatter.5.cloned.1.call-start = ((), (), s32[]{:S(2)}) async-start(), calls=%async_computation.3 | async-start | bytes 1064960 | tf_op jit(solution)/shard_map/reduce_scatter | solution.py:107
  184.1 0.8 copy-start.3
  357.1 4.0 copy-start.1
  363.4 3.2 copy-start
  373.9 3.2 copy-start
  384.4 3.2 copy-start
  394.9 3.2 copy-start
  970.7 33.8 %copy-start.9 = (u32[256]{0:T(256)S(1)}, u32[256]{0:T(256)}, u32[]{:S(2)}) copy-start(u32[256]{0:T(256)} %constant.110) | copy-start | bytes 3076
  970.7 35.1 %copy-start.8 = (s32[16]{0:T(128)S(1)}, s32[16]{0:T(128)}, u32[]{:S(2)}) copy-start(s32[16]{0:T(128)} %param.14) | copy-start | bytes 196
  974.3 2.8 copy-start.4
  982.5 3.2 copy-start.4
  991.0 3.2 copy-start.4
  999.5 3.2 copy-start.4
  1004.4 763.9 %reduce-scatter.3.cloned.1.call-start = ((), (), s32[]{:S(2)}) async-start(), calls=%async_computation.2 | async-start | bytes 1064960 | tf_op jit(solution)/shard_map/reduce_scatter | solution.py:108
  1055.4 7.0 copy-start.2
  1062.3 707.3 %all-reduce.3.cloned.1.call-start = ((), (), s32[]{:S(2)}) async-start(), calls=%async_computation.4 | async-start | bytes 4194304 | tf_op jit(solution)/shard_map/psum | solution.py:114
  1074.6 693.6 %copy-start.7 = (bf16[16,256]{1,0:T(8,128)(2,1)S(1)}, bf16[16,256]{1,0:T(8,128)(2,1)}, u32[]{:S(2)}) copy-start(bf16[16,256]{1,0:T(8,128)(2,1)} %param.12) | copy-start | bytes 24580
  1074.6 695.1 %copy-start.5 = (f32[1,1024,256]{2,1,0:T(8,128)S(1)}, f32[1,1024,256]{2,1,0:T(8,128)}, u32[]{:S(2)}) copy-start(f32[1,1024,256]{2,1,0:T(8,128)} %param.17) | copy-start | bytes 3145732
  1074.6 695.1 %copy-start.6 = (f32[1,1024,256]{2,1,0:T(8,128)S(1)}, f32[1,1024,256]{2,1,0:T(8,128)}, u32[]{:S(2)}) copy-start(f32[1,1024,256]{2,1,0:T(8,128)} %param.16) | copy-start | bytes 3145732
Sparse Core Ops, SparseCore 0:
  1004.5 382.0 reduce-scatter.4
  1389.8 378.3 reduce-scatter.2
Sparse Core Ops, SparseCore 1:
  1078.6 68.2 all-reduce.2
where the time goes:
time: 1820 us; the launch traced here: 1780 us
  blocking collectives  958 us (53%)
  waiting for transfers between devices  690 us (38%)
  other arithmetic  52.5 us (3%)
  matrix products  37.8 us (2%)
  local copies, waits for them, and re-layouts  22.5 us (1%)
    all_gather x3, blocking collectives, combined_all(): everything = jax.tree.map(lambda part: lax.all_gather(part, axis), shard)  560 us
    reduce_scatter x1, waiting for transfers between devices, per_device(): lax.psum_scatter(lookup, 'code', scatter_dimension=0, tiled=True)  382 us
    reduce_scatter x1, waiting for transfers between devices, per_device(): lax.psum_scatter(soft_grad, 'code', scatter_dimension=0, tiled=True)  308 us
    all_gather x1, blocking collectives, per_device(): lax.all_gather(latents, 'code', axis=0, tiled=True)  176 us
    all_gather x1, blocking collectives, per_device(): lax.all_gather(upstream, 'code', axis=0, tiled=True)  172 us
    unnamed x1, blocking collectives  49.4 us
  transfers between devices with their start and end apart: 3, of which 2 were waited for; matrix products, arithmetic and copies ran while one was open for 1% of the time, Pallas kernels for 0%

commit v1 on v0

v1 whole, which is shorter than its diff:
```python
import functools

import jax
import jax.numpy as jnp
from jax import lax
from jax.experimental import pallas as pl
from jax.experimental.pallas import tpu as pltpu
from jax.sharding import PartitionSpec as P

ADAM_STEP = 100
logit_scale = 4.0
commit_weight = 0.5
learn_rate = 0.001
beta_one = 0.9
beta_two = 0.999
adam_eps = 1e-08

NX, NY, NZ = 4, 4, 8
MESH = pl.DeviceIdType.MESH
LOG2E = 1.4426950408889634
SCALE = logit_scale * LOG2E
BF = jnp.bfloat16
F32 = jnp.float32


def rows_dot(lhs, rhs):
    return lax.dot_general(lhs, rhs, (((1,), (1,)), ((), ())), preferred_element_type=F32)


def plain_dot(lhs, rhs):
    return jnp.dot(lhs, rhs, preferred_element_type=F32)


def fold_rows(block, op):
    return op(block.reshape(block.shape[0] // 8, 8, block.shape[1]), axis=0)


def merge_stats(parts):
    peak = functools.reduce(jnp.maximum, [part[0] for part in parts])
    fades = [jnp.exp2((part[0] - peak) * SCALE) for part in parts]
    mass = sum(part[1] * fade for part, fade in zip(parts, fades))
    weighted = sum(part[2] * fade for part, fade in zip(parts, fades))
    return peak, mass, weighted


def kernel(
    chunk, stop,
    lat_ref, up_ref, tgt_ref, book_ref,
    quant_ref, grad_ref, code_ref,
    rows, tgt_z, tgt_all, wide, codes, codes_t, expo, aff, weights,
    soft_out, quant_out, rs_one, rs_two, rs_mid, rs_last, rs_three,
    stat_own, stat_x, stat_y, stat_z, stat_mid, stat_fin, code_out, code_in,
    load_sem, gz_s, gz_r, g2_s, g2_r, g3_s, g3_r, tz_s, tz_r, t2_s, t2_r, t3_s, t3_r,
    sx_s, sx_r, sy_s, sy_r, sz_s, sz_r, sf_s, sf_r,
    r1_s, r1_r, r2_s, r2_r, r3_s, r3_r, core_s, core_r,
):
    own_rows, channels = lat_ref.shape
    width = own_rows * NZ
    groups = NX * NY
    blocks = groups // 2
    span = codes.shape[0]
    half = span // 2
    high = NZ // 2
    dp, code = lax.axis_index("dp"), lax.axis_index("code")
    x, y = lax.div(code, NY * high), lax.rem(lax.div(code, high), NY)
    low, core = lax.div(dp, 2), lax.rem(dp, 2)
    z = lax.rem(code, high) * 2 + low

    def at_x(k):
        return lax.rem(x + k, NX)

    def at_y(k):
        return lax.rem(y + k, NY)

    def at_z(k):
        return lax.rem(z + k, NZ)

    def device(px, py, pz, pc):
        return (lax.rem(pz, 2) * 2 + pc, (px * NY + py) * high + lax.div(pz, 2))

    def to_x(k):
        return device(at_x(k), y, z, core)

    def to_y(k):
        return device(x, at_y(k), z, core)

    def to_z(k):
        return device(x, y, at_z(k), core)

    twin = device(x, y, z, 1 - core)
    sent = []

    def push(src, dst, send, recv, target):
        copy = pltpu.make_async_remote_copy(
            src_ref=src, dst_ref=dst, send_sem=send, recv_sem=recv,
            device_id=target, device_id_type=MESH,
        )
        copy.start()
        sent.append(copy)
        return copy

    def arrive(copies):
        for copy in copies:
            copy.wait_recv()

    load = pltpu.make_async_copy(
        book_ref.at[pl.ds(pl.multiple_of(low * span, span), span)], wide, load_sem
    )
    load.start()

    barrier = pltpu.get_barrier_semaphore()
    partners = (
        [to_x(k) for k in range(1, NX)]
        + [to_y(k) for k in range(1, NY)]
        + [to_z(k) for k in range(1, NZ)]
        + [twin]
    )
    for partner in partners:
        pl.semaphore_signal(barrier, inc=1, device_id=partner, device_id_type=MESH)
    pl.semaphore_wait(barrier, len(partners))

    rows[0, x, y, z] = lat_ref[...]
    rows[1, x, y, z] = up_ref[...]
    tgt_z[z] = tgt_ref[...]
    first = [
        push(tgt_z.at[z], tgt_z.at[z], tz_s.at[k], tz_r.at[k], to_z(k)) for k in range(1, NZ)
    ] + [
        push(rows.at[:, x, y, z], rows.at[:, x, y, z], gz_s.at[k], gz_r.at[k], to_z(k))
        for k in range(1, NZ)
    ]
    load.wait()
    codes[...] = wide[...].astype(BF)
    codes_t[...] = wide[...].T.astype(BF)
    arrive(first)
    tgt_all[x, y] = jnp.sum(tgt_z[...], axis=0)
    second = (
        [push(tgt_all.at[x, y], tgt_all.at[x, y], t2_s.at[k], t2_r.at[k], to_y(k)) for k in range(1, NY)]
        + [push(rows.at[0, x, y], rows.at[0, x, y], g2_s.at[0, k], g2_r.at[0, k], to_y(k)) for k in range(1, NY)]
        + [push(rows.at[1, x, y], rows.at[1, x, y], g2_s.at[1, k], g2_r.at[1, k], to_x(k)) for k in range(1, NX)]
    )
    arrive(second)
    third = (
        [push(tgt_all.at[x], tgt_all.at[x], t3_s.at[k], t3_r.at[k], to_x(k)) for k in range(1, NX)]
        + [push(rows.at[0, x], rows.at[0, x], g3_s.at[0, k], g3_r.at[0, k], to_x(k)) for k in range(1, NX)]
        + [push(rows.at[1, :, y], rows.at[1, :, y], g3_s.at[1, k], g3_r.at[1, k], to_y(k)) for k in range(1, NY)]
    )
    arrive(third)

    def place(b):
        return lax.div(b, NY // 2), lax.rem(b, NY // 2) * 2

    def row_block(part, b):
        px, py = place(b)
        return rows[part, px, pl.ds(py, 2)].reshape(2 * width, channels)

    def piece(c):
        return pl.ds(pl.multiple_of(c * chunk, chunk), chunk)

    def finish():
        for copy in sent:
            copy.wait_send()

    def leave():
        quant_ref[...] = rows[0, 0, 0, 0]
        grad_ref[...] = rows[1, 0, 0, 0].astype(F32)
        code_ref[...] = wide[pl.ds(0, half)]
        finish()

    if stop == 1:
        return leave()

    def local_stats(b, carry):
        px, py = place(b)
        lat_b = row_block(0, b)
        up_b = row_block(1, b)

        def scores(c, peak):
            s = rows_dot(codes[piece(c)], lat_b)
            expo[2 * b, piece(c)] = s[:, :width]
            expo[2 * b + 1, piece(c)] = s[:, width:]
            return jnp.maximum(peak, fold_rows(s, jnp.max))

        peak = lax.fori_loop(0, span // chunk, scores, jnp.full((8, 2 * width), -jnp.inf, F32))
        peak = jnp.max(peak, axis=0, keepdims=True)
        shift = peak * SCALE

        def sums(c, carry):
            mass, weighted = carry
            a = rows_dot(codes[piece(c)], up_b)
            s = jnp.concatenate([expo[2 * b, piece(c)], expo[2 * b + 1, piece(c)]], axis=1)
            e = jnp.exp2(s * SCALE - shift)
            expo[2 * b, piece(c)] = e[:, :width]
            expo[2 * b + 1, piece(c)] = e[:, width:]
            aff[2 * b, piece(c)] = a[:, :width]
            aff[2 * b + 1, piece(c)] = a[:, width:]
            return mass + fold_rows(e, jnp.sum), weighted + fold_rows(e * a, jnp.sum)

        zero = jnp.zeros((8, 2 * width), F32)
        mass, weighted = lax.fori_loop(0, span // chunk, sums, (zero, zero))
        mass = jnp.sum(mass, axis=0, keepdims=True)
        weighted = jnp.sum(weighted, axis=0, keepdims=True)
        for k, value in enumerate((peak, mass, weighted)):
            stat_own[px, k, py] = value[:, :width]
            stat_own[px, k, py + 1] = value[:, width:]
        return carry

    lax.fori_loop(0, blocks, local_stats, 0)
    if stop == 2:
        return leave()

    sx = [push(stat_own.at[at_x(k)], stat_x.at[x], sx_s.at[k], sx_r.at[k], to_x(k)) for k in range(1, NX)]

    def back_rows(out):
        def body(b, carry):
            px, py = place(b)
            pair = jnp.concatenate([weights[2 * b], weights[2 * b + 1]], axis=1)
            t = plain_dot(codes_t[...], pair).astype(BF)
            out[px, py] = t[:, :width]
            out[px, py + 1] = t[:, width:]
            return carry

        lax.fori_loop(0, blocks, body, 0)

    def back_codes(part, c):
        total = None
        for b in range(blocks):
            pair = jnp.concatenate([weights[2 * b, piece(c)], weights[2 * b + 1, piece(c)]], axis=1)
            term = plain_dot(pair, row_block(part, b))
            total = term if total is None else total + term
        return total

    base = code * (2 * span) + low * span

    def one_hot(b, carry):
        px, py = place(b)

        def body(c, carry):
            index = lax.broadcasted_iota(jnp.int32, (chunk, width), 0) + (base + c * chunk)
            for side in range(2):
                hit = index == tgt_all[px, py + side]
                weights[2 * b + side, piece(c)] = jnp.where(hit, 1.0, 0.0).astype(BF)
            return carry

        return lax.fori_loop(0, span // chunk, body, carry)

    lax.fori_loop(0, blocks, one_hot, 0)
    back_rows(quant_out)

    def picked(c, carry):
        wide[piece(c)] = back_codes(1, c)
        return carry

    lax.fori_loop(0, span // chunk, picked, 0)

    arrive(sx)
    merged = merge_stats([stat_own[x]] + [stat_x[at_x(k)] for k in range(1, NX)])
    for k in range(3):
        stat_mid[0, k] = merged[k]
    arrive([push(stat_mid.at[0], stat_y.at[y], sy_s.at[k], sy_r.at[k], to_y(k)) for k in range(1, NY)])
    merged = merge_stats([merged] + [stat_y[at_y(k)] for k in range(1, NY)])
    for k in range(3):
        stat_mid[1, k] = merged[k]
    arrive([push(stat_mid.at[1], stat_z.at[z], sz_s.at[k], sz_r.at[k], to_z(k)) for k in range(1, NZ)])
    peak, mass, weighted = merge_stats([merged] + [stat_z[at_z(k)] for k in range(1, NZ)])
    for k, value in enumerate((peak, logit_scale / mass, weighted / mass)):
        stat_fin[x, k] = value
    arrive([push(stat_fin.at[x], stat_fin.at[x], sf_s.at[k], sf_r.at[k], to_x(k)) for k in range(1, NX)])
    if stop == 3:
        return leave()

    def weigh(b, carry):
        px, py = place(b)
        fade = [
            jnp.exp2((stat_own[px, 0, py + side] - stat_fin[px, 0, py + side]) * SCALE)
            * stat_fin[px, 1, py + side]
            for side in range(2)
        ]
        mean = [stat_fin[px, 2, py + side] for side in range(2)]

        def body(c, carry):
            for side in range(2):
                w = expo[2 * b + side, piece(c)] * fade[side]
                w = w * (aff[2 * b + side, piece(c)] - mean[side])
                weights[2 * b + side, piece(c)] = w.astype(BF)
            return carry

        return lax.fori_loop(0, span // chunk, body, carry)

    lax.fori_loop(0, blocks, weigh, 0)
    back_rows(soft_out)

    side_c = channels // 2
    lower, upper = pl.ds(0, side_c), pl.ds(side_c, side_c)
    outs = (soft_out, quant_out)
    one = []
    for n, out in enumerate(outs):
        one += [push(out.at[at_x(k), :, lower], rs_one.at[n, 0, x], r1_s.at[n, 0, k], r1_r.at[n, 0, k], to_x(k)) for k in range(1, NX)]
        one += [push(out.at[:, at_y(k), upper], rs_one.at[n, 1, y], r1_s.at[n, 1, k], r1_r.at[n, 1, k], to_y(k)) for k in range(1, NY)]

    def grad_other(c, carry):
        at = (1 - core) * half + c * chunk
        code_out[piece(c)] = (back_codes_at(at) + wide[pl.ds(pl.multiple_of(at, chunk), chunk)]).astype(BF)
        return carry

    def back_codes_at(at):
        total = None
        where = pl.ds(pl.multiple_of(at, chunk), chunk)
        for b in range(blocks):
            pair = jnp.concatenate([weights[2 * b, where], weights[2 * b + 1, where]], axis=1)
            term = plain_dot(pair, row_block(0, b))
            total = term if total is None else total + term
        return total

    lax.fori_loop(0, half // chunk, grad_other, 0)
    swap = push(code_out, code_in, core_s, core_r, twin)

    def grad_own(c, carry):
        at = core * half + c * chunk
        code_ref[piece(c)] = back_codes_at(at) + wide[pl.ds(pl.multiple_of(at, chunk), chunk)]
        return carry

    lax.fori_loop(0, half // chunk, grad_own, 0)

    arrive(one)
    two = []
    for n, out in enumerate(outs):
        for j in range(NY):
            total = out[x, j, lower].astype(F32)
            for k in range(1, NX):
                total = total + rs_one[n, 0, at_x(k), j].astype(F32)
            rs_mid[n, 0, j] = total.astype(BF)
        for j in range(NX):
            total = out[j, y, upper].astype(F32)
            for k in range(1, NY):
                total = total + rs_one[n, 1, at_y(k), j].astype(F32)
            rs_mid[n, 1, j] = total.astype(BF)
        two += [push(rs_mid.at[n, 0, at_y(k)], rs_two.at[n, 0, y], r2_s.at[n, 0, k], r2_r.at[n, 0, k], to_y(k)) for k in range(1, NY)]
        two += [push(rs_mid.at[n, 1, at_x(k)], rs_two.at[n, 1, x], r2_s.at[n, 1, k], r2_r.at[n, 1, k], to_x(k)) for k in range(1, NX)]
    arrive(two)
    for n in range(2):
        left = rs_mid[n, 0, y].astype(F32)
        for k in range(1, NY):
            left = left + rs_two[n, 0, at_y(k)].astype(F32)
        right = rs_mid[n, 1, x].astype(F32)
        for k in range(1, NX):
            right = right + rs_two[n, 1, at_x(k)].astype(F32)
        total = jnp.concatenate([left, right], axis=0).T.astype(BF)
        rs_last[n] = total.reshape(NZ, own_rows, channels)
    three = [
        push(rs_last.at[:, at_z(k)], rs_three.at[:, z], r3_s.at[k], r3_r.at[k], to_z(k)) for k in range(1, NZ)
    ]
    swap.wait_recv()
    code_ref[...] = code_ref[...] + code_in[...].astype(F32)
    arrive(three)
    soft = rs_last[0, z].astype(F32)
    quant = rs_last[1, z].astype(F32)
    for k in range(1, NZ):
        soft = soft + rs_three[0, at_z(k)].astype(F32)
        quant = quant + rs_three[1, at_z(k)].astype(F32)
    quant_ref[...] = quant.astype(BF)
    grad_ref[...] = soft + commit_weight * (lat_ref[...].astype(F32) - quant)
    finish()


def exchange(latents, upstream, targets, codebook, stop=0):
    own_rows, channels = latents.shape
    width = own_rows * NZ
    span = codebook.shape[0] // 2
    half = span // 2
    groups = NX * NY
    chunk = min(512, half)
    z = lax.rem(lax.axis_index("code"), NZ // 2) * 2 + lax.div(lax.axis_index("dp"), 2)
    spread = jnp.where(jnp.arange(NZ)[:, None] == z, targets[None, :], 0).reshape(1, width)
    dma = pltpu.SemaphoreType.DMA
    side_c = channels // 2
    in_vmem = pl.BlockSpec(memory_space=pltpu.VMEM)
    scratch = [
        pltpu.VMEM((2, NX, NY, NZ, own_rows, channels), BF),
        pltpu.VMEM((NZ, 1, width), jnp.int32),
        pltpu.VMEM((NX, NY, 1, width), jnp.int32),
        pltpu.VMEM((span, channels), F32),
        pltpu.VMEM((span, channels), BF),
        pltpu.VMEM((channels, span), BF),
        pltpu.VMEM((groups, span, width), F32),
        pltpu.VMEM((groups, span, width), F32),
        pltpu.VMEM((groups, span, width), BF),
        pltpu.VMEM((NX, NY, channels, width), BF),
        pltpu.VMEM((NX, NY, channels, width), BF),
        pltpu.VMEM((2, 2, NX, NY, side_c, width), BF),
        pltpu.VMEM((2, 2, NX, side_c, width), BF),
        pltpu.VMEM((2, 2, NX, side_c, width), BF),
        pltpu.VMEM((2, NZ, own_rows, channels), BF),
        pltpu.VMEM((2, NZ, own_rows, channels), BF),
        pltpu.VMEM((NX, 3, NY, 1, width), F32),
        pltpu.VMEM((NX, 3, NY, 1, width), F32),
        pltpu.VMEM((NY, 3, NY, 1, width), F32),
        pltpu.VMEM((NZ, 3, NY, 1, width), F32),
        pltpu.VMEM((2, 3, NY, 1, width), F32),
        pltpu.VMEM((NX, 3, NY, 1, width), F32),
        pltpu.VMEM((half, channels), BF),
        pltpu.VMEM((half, channels), BF),
        dma,
        dma((NZ,)), dma((NZ,)), dma((2, NX)), dma((2, NX)), dma((2, NX)), dma((2, NX)),
        dma((NZ,)), dma((NZ,)), dma((NY,)), dma((NY,)), dma((NX,)), dma((NX,)),
        dma((NX,)), dma((NX,)), dma((NY,)), dma((NY,)), dma((NZ,)), dma((NZ,)), dma((NX,)), dma((NX,)),
        dma((2, 2, NX)), dma((2, 2, NX)), dma((2, 2, NX)), dma((2, 2, NX)), dma((NZ,)), dma((NZ,)),
        dma, dma,
    ]
    return pl.pallas_call(
        functools.partial(kernel, chunk, stop),
        out_shape=(
            jax.ShapeDtypeStruct((own_rows, channels), BF),
            jax.ShapeDtypeStruct((own_rows, channels), F32),
            jax.ShapeDtypeStruct((half, channels), F32),
        ),
        in_specs=[in_vmem, in_vmem, in_vmem, pl.BlockSpec(memory_space=pl.ANY)],
        out_specs=(in_vmem, in_vmem, in_vmem),
        scratch_shapes=scratch,
        compiler_params=pltpu.CompilerParams(
            collective_id=0, has_side_effects=True, vmem_limit_bytes=60 * 1024 * 1024
        ),
    )(latents, upstream, spread, codebook)


def per_device(latents, upstream, targets, codebook, moment_one, moment_two, stop=0):
    quantized, latent_grad, code_grad = exchange(latents, upstream, targets, codebook, stop)
    quarter = code_grad.shape[0]
    own_codes = lax.dynamic_slice_in_dim(codebook, lax.axis_index("dp") * quarter, quarter, 0)
    fresh_one = beta_one * moment_one[0] + (1.0 - beta_one) * code_grad
    fresh_two = beta_two * moment_two[0] + (1.0 - beta_two) * code_grad * code_grad
    fix_one = 1.0 - beta_one**ADAM_STEP
    fix_two = 1.0 - beta_two**ADAM_STEP
    updated = own_codes - learn_rate * (fresh_one / fix_one) / (
        jnp.sqrt(fresh_two / fix_two) + adam_eps
    )
    return (quantized, latent_grad, updated[None], fresh_one[None], fresh_two[None])


def solution(mesh, stop=0):
    return jax.shard_map(
        functools.partial(per_device, stop=stop),
        mesh=mesh,
        in_specs=(
            P(("dp", "code"), None),
            P(("dp", "code"), None),
            P(("dp", "code")),
            P("code", None),
            P("code", "dp", None),
            P("code", "dp", None),
        ),
        out_specs=(
            P(("dp", "code"), None),
            P(("dp", "code"), None),
            P("code", "dp", None),
            P("code", "dp", None),
            P("code", "dp", None),
        ),
        check_vma=False,
    )
```

time: 1820 us -> 109 us (0.06); the launches traced: 1780 us -> 108 us
  blocking collectives: 958 us -> 0 us
  waiting for transfers between devices: 690 us -> 0 us
  Pallas kernels: 0 us -> 101 us
  other arithmetic: 52.5 us -> 4.76 us
  matrix products: 37.8 us -> 0 us
  local copies, waits for them, and re-layouts: 22.5 us -> 1.81 us
    all_gather x5 -> x0, blocking collectives: 909 us -> none  [the longest x3 560 us: combined_all(): everything = jax.tree.map(lambda part: lax.all_gather(part, axis), shard)]
    reduce_scatter x2 -> x0, waiting for transfers between devices: 690 us -> none  [the longest x1 382 us: per_device(): lax.psum_scatter(lookup, 'code', scatter_dimension=0, tiled=True)]
    pallas_call x0 -> x1, Pallas kernels: none -> 101 us  [exchange(): pl.pallas_call(functools.partial(kernel, chunk, stop), out_shape=(jax.Sha...]
    unnamed x1 -> x0, blocking collectives: 49.4 us -> none
    dot_general x16 -> x0, matrix products: 37.8 us -> none  [the longest x8 18.6 us: score_pair(): lax.dot_general(stacked, code_block, (((1,), (1,)), ((), ())), preferred_...]
  transfers between devices with their start and end apart: 3 -> 0, of which waited for: 2 -> 0; matrix products, arithmetic and copies ran while one was open for 1% -> 0% of each run, Pallas kernels for 0% -> 0%
where the time goes in v1:
time: 109 us; the launch traced here: 108 us
  Pallas kernels  101 us (93%)
  other arithmetic  4.76 us (4%)
  local copies, waits for them, and re-layouts  1.81 us (2%)
    pallas_call x1, Pallas kernels, exchange(): pl.pallas_call(functools.partial(kernel, chunk, stop), out_shape=(jax.Sha...  101 us
    broadcast_in_dim x1, other arithmetic, per_device(): fresh_two[None]  3.88 us

profile of v1, /device:TPU:2, one launch (start us, length us, event | category | flops | bytes accessed | tf_op | source)
XLA Modules:
  0.0 108.3 jit_solution(6794359758122119069)
XLA Ops:
  0.6 0.0 copy-start
  0.6 0.0 copy-start.1
  0.7 0.9 broadcast_select_fusion
  1.5 0.6 select_n.18.tgt_ref
  2.1 101.1 %shard_map.101 = (bf16[16,256]{1,0:T(8,128)(2,1)}, f32[16,256]{1,0:T(8,128)}, f32[1024,256]{1,0:T(8,128)}) custom-call(bf16[16,256]{1,0:T(8,128)(2,1)} %lat_ref.1, bf16[16,256]{1,0:T(8,128)(2,1)} %up_ref.1, s32[1,128]{1,0:T(1,128)} %select_n.18.tgt_ref, f32[4096,256]{1,0:T(8,128)} %book_ref.1), custom_call_target="tpu_custom_call" | custom-call | tf_op jit(solution)/shard_map/pallas_call | solution.py:409
  103.2 0.0 copy-start.3
  103.2 0.0 copy-start.2
  103.2 0.0 copy-done
  103.2 0.0 copy-done.1
  103.2 3.9 %fusion.2 = (f32[1,1024,256]{2,1,0:T(8,128)}, f32[1,1024,256]{2,1,0:T(8,128)}, f32[1,1024,256]{2,1,0:T(8,128)}) fusion(f32[1024,256]{1,0:T(8,128)} %get-tuple-element.10, f32[1,1024,256]{2,1,0:T(8,128)S(1)} %copy-done, f32[1,1024,256]{2,1,0:T(8,128)S(1)} %copy-done.1, f32[4096,256]{1,0:T(8,128)} %book_ref.1, s32[]{:T(128)S(6)} %select_n.19), kind=kLoop, calls=%fused_computation.5 | loop fusion | flops 3145728 | bytes 7340036 | tf_op jit(solution)/shard_map/broadcast_in_dim | solution.py:436
  107.1 0.0 copy-done.3
  107.1 0.6 copy.13
  107.7 0.0 copy-done.2
  107.7 0.6 copy.14
  (1 shorter events, 0.0 us)
Async XLA Ops:
  0.6 102.6 %copy-start = (f32[1,1024,256]{2,1,0:T(8,128)S(1)}, f32[1,1024,256]{2,1,0:T(8,128)}, u32[]{:S(2)}) copy-start(f32[1,1024,256]{2,1,0:T(8,128)} %param.11) | copy-start | bytes 3145732
  0.6 102.6 %copy-start.1 = (f32[1,1024,256]{2,1,0:T(8,128)S(1)}, f32[1,1024,256]{2,1,0:T(8,128)}, u32[]{:S(2)}) copy-start(f32[1,1024,256]{2,1,0:T(8,128)} %param.10) | copy-start | bytes 3145732
  103.2 3.9 %copy-start.3 = (bf16[16,256]{1,0:T(8,128)(2,1)S(1)}, bf16[16,256]{1,0:T(8,128)(2,1)}, u32[]{:S(2)}) copy-start(bf16[16,256]{1,0:T(8,128)(2,1)} %get-tuple-element.19) | copy-start | bytes 24580
  103.2 4.5 %copy-start.2 = (f32[16,256]{1,0:T(8,128)S(1)}, f32[16,256]{1,0:T(8,128)}, u32[]{:S(2)}) copy-start(f32[16,256]{1,0:T(8,128)} %get-tuple-element.20) | copy-start | bytes 49156

commit v2 on v1

v2 whole, which is shorter than its diff:
```python
import functools

import jax
import jax.numpy as jnp
from jax import lax
from jax.experimental import pallas as pl
from jax.experimental.pallas import tpu as pltpu
from jax.sharding import PartitionSpec as P

ADAM_STEP = 100
logit_scale = 4.0
commit_weight = 0.5
learn_rate = 0.001
beta_one = 0.9
beta_two = 0.999
adam_eps = 1e-08

NX, NY, NZ = 4, 4, 8
MESH = pl.DeviceIdType.MESH
LOG2E = 1.4426950408889634
SCALE = logit_scale * LOG2E
BF = jnp.bfloat16
F32 = jnp.float32


def rows_dot(lhs, rhs):
    return lax.dot_general(lhs, rhs, (((1,), (1,)), ((), ())), preferred_element_type=F32)


def plain_dot(lhs, rhs):
    return jnp.dot(lhs, rhs, preferred_element_type=F32)


def fold_rows(block, op):
    return op(block.reshape(block.shape[0] // 16, 16, block.shape[1]), axis=0)


def merge_stats(parts):
    peak = functools.reduce(jnp.maximum, [part[0] for part in parts])
    fades = [jnp.exp2((part[0] - peak) * SCALE) for part in parts]
    mass = sum(part[1] * fade for part, fade in zip(parts, fades))
    weighted = sum(part[2] * fade for part, fade in zip(parts, fades))
    return peak, mass, weighted


def kernel(
    chunk,
    lat_ref, up_ref, tgt_ref, book_ref,
    terms_ref, code_ref,
    rows, tgt_z, tgt_all, wide, codes, codes_t, expo, aff, weights,
    soft_out, quant_out, rs_one, rs_two, rs_mid, rs_last, rs_three,
    stat_own, stat_x, stat_y, stat_z, stat_mid, stat_fin, code_out, code_in,
    load_sem, gz_s, gz_r, g2_s, g2_r, g3_s, g3_r, tz_s, tz_r, t2_s, t2_r, t3_s, t3_r,
    sx_s, sx_r, sy_s, sy_r, sz_s, sz_r, sf_s, sf_r,
    rx_s, rx_r, ry_s, ry_r, r2_s, r2_r, r3_s, r3_r, core_s, core_r,
):
    own_rows, channels = lat_ref.shape
    width = own_rows * NZ
    groups = NX * NY
    blocks = groups // 2
    span = codes.shape[0]
    half = span // 2
    high = NZ // 2
    dp, code = lax.axis_index("dp"), lax.axis_index("code")
    x, y = lax.div(code, NY * high), lax.rem(lax.div(code, high), NY)
    low, core = lax.div(dp, 2), lax.rem(dp, 2)
    z = lax.rem(code, high) * 2 + low

    def at_x(k):
        return lax.rem(x + k, NX)

    def at_y(k):
        return lax.rem(y + k, NY)

    def at_z(k):
        return lax.rem(z + k, NZ)

    def device(px, py, pz, pc):
        return (lax.rem(pz, 2) * 2 + pc, (px * NY + py) * high + lax.div(pz, 2))

    def to_x(k):
        return device(at_x(k), y, z, core)

    def to_y(k):
        return device(x, at_y(k), z, core)

    def to_z(k):
        return device(x, y, at_z(k), core)

    twin = device(x, y, z, 1 - core)
    sent = []

    def push(src, dst, send, recv, target):
        copy = pltpu.make_async_remote_copy(
            src_ref=src, dst_ref=dst, send_sem=send, recv_sem=recv,
            device_id=target, device_id_type=MESH,
        )
        copy.start()
        sent.append(copy)
        return copy

    def arrive(copies):
        for copy in copies:
            copy.wait_recv()

    load = pltpu.make_async_copy(
        book_ref.at[pl.ds(pl.multiple_of(low * span, span), span)], wide, load_sem
    )
    load.start()

    barrier = pltpu.get_barrier_semaphore()
    partners = (
        [to_z(k) for k in range(1, NZ)]
        + [to_x(k) for k in range(1, NX)]
        + [to_y(k) for k in range(1, NY)]
        + [twin]
    )
    for partner in partners:
        pl.semaphore_signal(barrier, inc=1, device_id=partner, device_id_type=MESH)

    rows[0, x, y, z] = lat_ref[...]
    rows[1, x, y, z] = up_ref[...]
    lane = lax.broadcasted_iota(jnp.int32, (1, width), 1) - z * own_rows
    own_targets = jnp.zeros((1, width), jnp.int32)
    for k in range(own_rows):
        own_targets = jnp.where(lane == k, tgt_ref[k], own_targets)
    tgt_z[z] = own_targets
    pl.semaphore_wait(barrier, len(partners))

    far_first = sorted(range(1, NZ), key=lambda k: -min(k, NZ - k))
    first = [
        push(rows.at[:, x, y, z], rows.at[:, x, y, z], gz_s.at[k], gz_r.at[k], to_z(k))
        for k in far_first
    ] + [
        push(tgt_z.at[z], tgt_z.at[z], tz_s.at[k], tz_r.at[k], to_z(k)) for k in far_first
    ]
    load.wait()
    codes[...] = wide[...].astype(BF)
    codes_t[...] = wide[...].T.astype(BF)
    arrive(first)
    tgt_all[x, y] = jnp.sum(tgt_z[...], axis=0)
    second = (
        [push(tgt_all.at[x, y], tgt_all.at[x, y], t2_s.at[k], t2_r.at[k], to_y(k)) for k in range(1, NY)]
        + [push(rows.at[0, x, y], rows.at[0, x, y], g2_s.at[0, k], g2_r.at[0, k], to_y(k)) for k in range(1, NY)]
        + [push(rows.at[1, x, y], rows.at[1, x, y], g2_s.at[1, k], g2_r.at[1, k], to_x(k)) for k in range(1, NX)]
    )
    arrive(second)
    third_tgt = [push(tgt_all.at[x], tgt_all.at[x], t3_s.at[k], t3_r.at[k], to_x(k)) for k in range(1, NX)]
    third_lat, third_up = {}, {}
    for k in (1, NX - 1, 2) if NX > 2 else (1,):
        third_lat[k] = push(rows.at[0, x], rows.at[0, x], g3_s.at[0, k], g3_r.at[0, k], to_x(k))
        third_up[k] = push(rows.at[1, :, y], rows.at[1, :, y], g3_s.at[1, k], g3_r.at[1, k], to_y(k))

    pairs = NY // 2

    def row_block(part, px, py):
        return rows[part, px, pl.ds(py, 2)].reshape(2 * width, channels)

    def piece(c):
        return pl.ds(c * chunk, chunk)

    pieces = span // chunk

    def scores(px):
        def body(j, carry):
            py = j * 2
            g = px * NY + py
            lat_b = row_block(0, px, py)
            peak = jnp.full((16, 2 * width), -jnp.inf, F32)
            for c in range(pieces):
                s = rows_dot(codes[piece(c)], lat_b)
                expo[g, piece(c)] = s[:, :width]
                expo[g + 1, piece(c)] = s[:, width:]
                peak = jnp.maximum(peak, fold_rows(s, jnp.max))
            peak = jnp.max(peak, axis=0, keepdims=True)
            stat_own[px, 0, py] = peak[:, :width]
            stat_own[px, 0, py + 1] = peak[:, width:]
            return carry

        lax.fori_loop(0, pairs, body, 0)

    def sums(b, carry):
        px, py = lax.div(b, pairs), lax.rem(b, pairs) * 2
        up_b = row_block(1, px, py)
        shift = jnp.concatenate([stat_own[px, 0, py], stat_own[px, 0, py + 1]], axis=1) * SCALE
        mass = jnp.zeros((16, 2 * width), F32)
        weighted = jnp.zeros((16, 2 * width), F32)
        for c in range(pieces):
            a = rows_dot(codes[piece(c)], up_b)
            s = jnp.concatenate([expo[2 * b, piece(c)], expo[2 * b + 1, piece(c)]], axis=1)
            e = jnp.exp2(s * SCALE - shift)
            expo[2 * b, piece(c)] = e[:, :width]
            expo[2 * b + 1, piece(c)] = e[:, width:]
            aff[2 * b, piece(c)] = a[:, :width]
            aff[2 * b + 1, piece(c)] = a[:, width:]
            mass = mass + fold_rows(e, jnp.sum)
            weighted = weighted + fold_rows(e * a, jnp.sum)
        mass = jnp.sum(mass, axis=0, keepdims=True)
        weighted = jnp.sum(weighted, axis=0, keepdims=True)
        for k, value in enumerate((mass, weighted)):
            stat_own[px, k + 1, py] = value[:, :width]
            stat_own[px, k + 1, py + 1] = value[:, width:]
        return carry

    def back_rows(out, px, py):
        g = px * NY + py
        pair = jnp.concatenate([weights[g], weights[g + 1]], axis=1)
        t = plain_dot(codes_t[...], pair).astype(BF)
        out[px, py] = t[:, :width]
        out[px, py + 1] = t[:, width:]

    def back_codes(part, at):
        where = pl.ds(pl.multiple_of(at, chunk), chunk)
        total = None
        for b in range(blocks):
            pair = jnp.concatenate([weights[2 * b, where], weights[2 * b + 1, where]], axis=1)
            term = plain_dot(pair, row_block(part, b // pairs, b % pairs * 2))
            total = term if total is None else total + term
        return total

    base = code * (2 * span) + low * span
    index = lax.broadcasted_iota(jnp.int32, (chunk, width), 0)

    def one_hot(b, carry):
        px, py = lax.div(b, pairs), lax.rem(b, pairs) * 2
        for side in range(2):
            local = tgt_all[px, py + side] - base
            for c in range(pieces):
                weights[2 * b + side, piece(c)] = jnp.where(index == local - c * chunk, 1.0, 0.0).astype(BF)
        back_rows(quant_out, px, py)
        return carry

    side_c = channels // 2
    lower, upper = pl.ds(0, side_c), pl.ds(side_c, side_c)

    def send_plane(n, out, k):
        px = at_x(k)
        copies = []
        if k:
            copies.append(push(out.at[px, :, lower], rs_one.at[n, 0, x], rx_s.at[n, k], rx_r.at[n, k], to_x(k)))
        for j in range(1, NY):
            copies.append(
                push(out.at[px, at_y(j), upper], rs_one.at[n, 1, y, px], ry_s.at[n, k, j], ry_r.at[n, k, j], to_y(j))
            )
        return copies

    def reduce_one(n, out):
        for j in range(NY):
            total = out[x, j, lower].astype(F32)
            for k in range(1, NX):
                total = total + rs_one[n, 0, at_x(k), j].astype(F32)
            rs_mid[n, 0, j] = total.astype(BF)
        copies = [
            push(rs_mid.at[n, 0, at_y(k)], rs_two.at[n, 0, y], r2_s.at[n, 0, k], r2_r.at[n, 0, k], to_y(k))
            for k in range(1, NY)
        ]
        for j in range(NX):
            total = out[j, y, upper].astype(F32)
            for k in range(1, NY):
                total = total + rs_one[n, 1, at_y(k), j].astype(F32)
            rs_mid[n, 1, j] = total.astype(BF)
        return copies + [
            push(rs_mid.at[n, 1, at_x(k)], rs_two.at[n, 1, x], r2_s.at[n, 1, k], r2_r.at[n, 1, k], to_x(k))
            for k in range(1, NX)
        ]

    def reduce_two(n):
        left = rs_mid[n, 0, y].astype(F32)
        for k in range(1, NY):
            left = left + rs_two[n, 0, at_y(k)].astype(F32)
        right = rs_mid[n, 1, x].astype(F32)
        for k in range(1, NX):
            right = right + rs_two[n, 1, at_x(k)].astype(F32)
        total = jnp.concatenate([left, right], axis=0).T.astype(BF)
        rs_last[n] = total.reshape(NZ, own_rows, channels)
        return [
            push(rs_last.at[n, at_z(k)], rs_three.at[n, z], r3_s.at[n, k], r3_r.at[n, k], to_z(k))
            for k in far_first
        ]

    def reduce_three(n):
        total = rs_last[n, z].astype(F32)
        for k in range(1, NZ):
            total = total + rs_three[n, at_z(k)].astype(F32)
        return total

    arrive(third_tgt)
    lax.fori_loop(0, blocks, one_hot, 0)
    scores(x)
    for k in third_lat:
        arrive([third_lat[k]])
        scores(at_x(NX - k))
    arrive(third_up.values())
    quant_one = []
    for k in (2, 1, 3, 0) if NX > 2 else (1, 0):
        quant_one += send_plane(1, quant_out, k)
    lax.fori_loop(0, blocks, sums, 0)

    sx = [push(stat_own.at[at_x(k)], stat_x.at[x], sx_s.at[k], sx_r.at[k], to_x(k)) for k in range(1, NX)]

    def picked(c, carry):
        at = c * chunk
        wide[pl.ds(pl.multiple_of(at, chunk), chunk)] = back_codes(1, at)
        return carry

    lax.fori_loop(0, pieces, picked, 0)
    arrive(sx)
    merged = merge_stats([stat_own[x]] + [stat_x[at_x(k)] for k in range(1, NX)])
    for k in range(3):
        stat_mid[0, k] = merged[k]
    sy = [push(stat_mid.at[0], stat_y.at[y], sy_s.at[k], sy_r.at[k], to_y(k)) for k in range(1, NY)]
    arrive(quant_one)
    quant_two = reduce_one(1, quant_out)
    arrive(sy)
    merged = merge_stats([merged] + [stat_y[at_y(k)] for k in range(1, NY)])
    for k in range(3):
        stat_mid[1, k] = merged[k]
    sz = [push(stat_mid.at[1], stat_z.at[z], sz_s.at[k], sz_r.at[k], to_z(k)) for k in far_first]
    arrive(quant_two)
    quant_three = reduce_two(1)
    arrive(sz)
    peak, mass, weighted = merge_stats([merged] + [stat_z[at_z(k)] for k in range(1, NZ)])
    for k, value in enumerate((peak, logit_scale / mass, weighted / mass)):
        stat_fin[x, k] = value
    arrive([push(stat_fin.at[x], stat_fin.at[x], sf_s.at[k], sf_r.at[k], to_x(k)) for k in range(1, NX)])

    def weigh(px):
        def body(j, carry):
            py = j * 2
            g = px * NY + py
            for side in range(2):
                fade = (
                    jnp.exp2((stat_own[px, 0, py + side] - stat_fin[px, 0, py + side]) * SCALE)
                    * stat_fin[px, 1, py + side]
                )
                mean = stat_fin[px, 2, py + side]
                for c in range(pieces):
                    w = expo[g + side, piece(c)] * fade * (aff[g + side, piece(c)] - mean)
                    weights[g + side, piece(c)] = w.astype(BF)
            back_rows(soft_out, px, py)
            return carry

        lax.fori_loop(0, pairs, body, 0)

    soft_one = []
    for k in (2, 1, 3, 0) if NX > 2 else (1, 0):
        weigh(at_x(k))
        soft_one += send_plane(0, soft_out, k)

    def grad_other(c, carry):
        at = (1 - core) * half + c * chunk
        where = pl.ds(pl.multiple_of(at, chunk), chunk)
        code_out[pl.ds(pl.multiple_of(c * chunk, chunk), chunk)] = (back_codes(0, at) + wide[where]).astype(BF)
        return carry

    lax.fori_loop(0, half // chunk, grad_other, 0)
    swap = push(code_out, code_in, core_s, core_r, twin)
    arrive(soft_one)
    soft_two = reduce_one(0, soft_out)

    def grad_own(c, carry):
        at = core * half + c * chunk
        where = pl.ds(pl.multiple_of(at, chunk), chunk)
        code_ref[pl.ds(pl.multiple_of(c * chunk, chunk), chunk)] = back_codes(0, at) + wide[where]
        return carry

    lax.fori_loop(0, half // chunk, grad_own, 0)
    arrive(soft_two)
    soft_three = reduce_two(0)
    swap.wait_recv()
    code_ref[...] = code_ref[...] + code_in[...].astype(F32)
    arrive(quant_three)
    terms_ref[1] = reduce_three(1)
    arrive(soft_three)
    terms_ref[0] = reduce_three(0)
    for copy in sent:
        copy.wait_send()


def exchange(latents, upstream, targets, codebook):
    own_rows, channels = latents.shape
    width = own_rows * NZ
    span = codebook.shape[0] // 2
    half = span // 2
    groups = NX * NY
    chunk = min(256, half)
    dma = pltpu.SemaphoreType.DMA
    side_c = channels // 2
    in_vmem = pl.BlockSpec(memory_space=pltpu.VMEM)
    scratch = [
        pltpu.VMEM((2, NX, NY, NZ, own_rows, channels), BF),
        pltpu.VMEM((NZ, 1, width), jnp.int32),
        pltpu.VMEM((NX, NY, 1, width), jnp.int32),
        pltpu.VMEM((span, channels), F32),
        pltpu.VMEM((span, channels), BF),
        pltpu.VMEM((channels, span), BF),
        pltpu.VMEM((groups, span, width), F32),
        pltpu.VMEM((groups, span, width), F32),
        pltpu.VMEM((groups, span, width), BF),
        pltpu.VMEM((NX, NY, channels, width), BF),
        pltpu.VMEM((NX, NY, channels, width), BF),
        pltpu.VMEM((2, 2, NX, NY, side_c, width), BF),
        pltpu.VMEM((2, 2, NX, side_c, width), BF),
        pltpu.VMEM((2, 2, NX, side_c, width), BF),
        pltpu.VMEM((2, NZ, own_rows, channels), BF),
        pltpu.VMEM((2, NZ, own_rows, channels), BF),
        pltpu.VMEM((NX, 3, NY, 1, width), F32),
        pltpu.VMEM((NX, 3, NY, 1, width), F32),
        pltpu.VMEM((NY, 3, NY, 1, width), F32),
        pltpu.VMEM((NZ, 3, NY, 1, width), F32),
        pltpu.VMEM((2, 3, NY, 1, width), F32),
        pltpu.VMEM((NX, 3, NY, 1, width), F32),
        pltpu.VMEM((half, channels), BF),
        pltpu.VMEM((half, channels), BF),
        dma,
        dma((NZ,)), dma((NZ,)), dma((2, NX)), dma((2, NX)), dma((2, NX)), dma((2, NX)),
        dma((NZ,)), dma((NZ,)), dma((NY,)), dma((NY,)), dma((NX,)), dma((NX,)),
        dma((NX,)), dma((NX,)), dma((NY,)), dma((NY,)), dma((NZ,)), dma((NZ,)), dma((NX,)), dma((NX,)),
        dma((2, NX)), dma((2, NX)), dma((2, NX, NY)), dma((2, NX, NY)),
        dma((2, 2, NX)), dma((2, 2, NX)), dma((2, NZ)), dma((2, NZ)),
        dma, dma,
    ]
    return pl.pallas_call(
        functools.partial(kernel, chunk),
        out_shape=(
            jax.ShapeDtypeStruct((2, own_rows, channels), F32),
            jax.ShapeDtypeStruct((half, channels), F32),
        ),
        in_specs=[in_vmem, in_vmem, pl.BlockSpec(memory_space=pltpu.SMEM), pl.BlockSpec(memory_space=pl.ANY)],
        out_specs=(in_vmem, in_vmem),
        scratch_shapes=scratch,
        compiler_params=pltpu.CompilerParams(
            collective_id=0, has_side_effects=True, vmem_limit_bytes=60 * 1024 * 1024
        ),
    )(latents, upstream, targets, codebook)


def finish(terms, lat, grad, book, one, two, quant_ref, lat_ref, book_ref, one_ref, two_ref, held, sem_in, sem_out):
    quarter = grad.shape[0]
    steps = 4
    size = quarter // steps
    own = lax.axis_index("dp") * quarter
    sources = (grad, book, one.at[0], two.at[0])
    targets = (book_ref.at[0], one_ref.at[0], two_ref.at[0])
    fix_one = 1.0 - beta_one**ADAM_STEP
    fix_two = 1.0 - beta_two**ADAM_STEP

    def fetch(n, c):
        start = own + c * size if n == 1 else c * size
        where = pl.ds(pl.multiple_of(start, size), size)
        return pltpu.make_async_copy(sources[n].at[where], held.at[n, pl.ds(c * size, size)], sem_in.at[n, c])

    def put(n, c):
        where = pl.ds(c * size, size)
        return pltpu.make_async_copy(held.at[4 + n, where], targets[n].at[where], sem_out.at[n, c])

    for c in range(steps):
        for n in range(4):
            fetch(n, c).start()
    quant = terms[1]
    quant_ref[...] = quant.astype(BF)
    lat_ref[...] = terms[0] + commit_weight * (lat[...].astype(F32) - quant)
    for c in range(steps):
        for n in range(4):
            fetch(n, c).wait()
        where = pl.ds(c * size, size)
        slope = held[0, where]
        fresh_one = beta_one * held[2, where] + (1.0 - beta_one) * slope
        fresh_two = beta_two * held[3, where] + (1.0 - beta_two) * slope * slope
        held[5, where] = fresh_one
        held[6, where] = fresh_two
        held[4, where] = held[1, where] - learn_rate * (fresh_one / fix_one) / (
            jnp.sqrt(fresh_two / fix_two) + adam_eps
        )
        for n in range(3):
            put(n, c).start()
    for c in range(steps):
        for n in range(3):
            put(n, c).wait()


def per_device(latents, upstream, targets, codebook, moment_one, moment_two):
    terms, code_grad = exchange(latents, upstream, targets, codebook)
    quarter, channels = code_grad.shape
    in_vmem = pl.BlockSpec(memory_space=pltpu.VMEM)
    anywhere = pl.BlockSpec(memory_space=pl.ANY)
    moment = jax.ShapeDtypeStruct(moment_one.shape, F32)
    return pl.pallas_call(
        finish,
        out_shape=(
            jax.ShapeDtypeStruct(latents.shape, BF),
            jax.ShapeDtypeStruct(latents.shape, F32),
            moment, moment, moment,
        ),
        in_specs=[in_vmem, in_vmem, anywhere, anywhere, anywhere, anywhere],
        out_specs=(in_vmem, in_vmem, anywhere, anywhere, anywhere),
        scratch_shapes=[
            pltpu.VMEM((7, quarter, channels), F32),
            pltpu.SemaphoreType.DMA((4, 4)),
            pltpu.SemaphoreType.DMA((3, 4)),
        ],
        compiler_params=pltpu.CompilerParams(vmem_limit_bytes=60 * 1024 * 1024),
    )(terms, latents, code_grad, codebook, moment_one, moment_two)


def solution(mesh):
    return jax.shard_map(
        per_device,
        mesh=mesh,
        in_specs=(
            P(("dp", "code"), None),
            P(("dp", "code"), None),
            P(("dp", "code")),
            P("code", None),
            P("code", "dp", None),
            P("code", "dp", None),
        ),
        out_specs=(
            P(("dp", "code"), None),
            P(("dp", "code"), None),
            P("code", "dp", None),
            P("code", "dp", None),
            P("code", "dp", None),
        ),
        check_vma=False,
    )
```

time: 109 us -> 82.9 us (0.76)
  Pallas kernels: 101 us -> 81.9 us
  other arithmetic: 4.76 us -> 0 us
  local copies, waits for them, and re-layouts: 1.81 us -> 0 us
    pallas_call x1 -> x2, Pallas kernels: 101 us -> 81.9 us  [the longest x1 77.1 us: exchange(): pl.pallas_call(functools.partial(kernel, chunk), out_shape=(jax.ShapeDtyp...]
    broadcast_in_dim x1 -> x0, other arithmetic: 3.88 us -> none  [per_device(): fresh_two[None]]
    unnamed x10 -> x0, local copies, waits for them, and re-layouts: 1.22 us -> none
where the time goes in v2:
time: 82.9 us; the launch traced here: 82.6 us
  Pallas kernels  81.9 us (99%)
    pallas_call x1, Pallas kernels, exchange(): pl.pallas_call(functools.partial(kernel, chunk), out_shape=(jax.ShapeDtyp...  77.1 us
    pallas_call x1, Pallas kernels, per_device(): pl.pallas_call(finish, out_shape=(jax.ShapeDtypeStruct(latents.shape, BF)...  4.88 us

profile of v2, /device:TPU:2, one launch (start us, length us, event | category | flops | bytes accessed | tf_op | source)
XLA Modules:
  0.0 82.6 jit_solution(2501408280179409112)
XLA Ops:
  0.6 77.1 %shard_map.101 = (f32[2,16,256]{2,1,0:T(8,128)}, f32[1024,256]{1,0:T(8,128)}) custom-call(bf16[16,256]{1,0:T(8,128)(2,1)} %lat.1, bf16[16,256]{1,0:T(8,128)(2,1)} %up_ref.1, s32[16]{0:T(128)} %tgt_ref.1, f32[4096,256]{1,0:T(8,128)} %book.1), custom_call_target="tpu_custom_call" | custom-call | tf_op jit(solution)/shard_map/pallas_call | solution.py:423
  77.7 4.9 %shard_map.102 = (bf16[16,256]{1,0:T(8,128)(2,1)}, f32[16,256]{1,0:T(8,128)}, f32[1,1024,256]{2,1,0:T(8,128)}, f32[1,1024,256]{2,1,0:T(8,128)}, f32[1,1024,256]{2,1,0:T(8,128)}) custom-call(f32[2,16,256]{2,1,0:T(8,128)} %get-tuple-element.7.terms, bf16[16,256]{1,0:T(8,128)(2,1)} %lat.1, f32[1024,256]{1,0:T(8,128)} %get-tuple-element.8.grad, ...), custom_call_target="tpu_custom_call" | custom-call | tf_op jit(solution)/shard_map/pallas_call | solution.py:488

commit v3 on v2

--- a/solution.py
+++ b/solution.py
@@ -45,12 +45,12 @@
 
 def kernel(
     chunk,
-    lat_ref, up_ref, tgt_ref, book_ref,
-    terms_ref, code_ref,
+    lat_ref, up_ref, tgt_ref, book_ref, one_ref, two_ref,
+    terms_ref, adam,
     rows, tgt_z, tgt_all, wide, codes, codes_t, expo, aff, weights,
     soft_out, quant_out, rs_one, rs_two, rs_mid, rs_last, rs_three,
-    stat_own, stat_x, stat_y, stat_z, stat_mid, stat_fin, code_out, code_in,
-    load_sem, gz_s, gz_r, g2_s, g2_r, g3_s, g3_r, tz_s, tz_r, t2_s, t2_r, t3_s, t3_r,
+    stat_own, stat_x, stat_y, stat_z, stat_mid, stat_fin, code_out, code_in, own_grad,
+    load_sem, adam_s, gz_s, gz_r, g2_s, g2_r, gx_s, gx_r, tz_s, tz_r, t2_s, t2_r, t3_s, t3_r,
     sx_s, sx_r, sy_s, sy_r, sz_s, sz_r, sf_s, sf_r,
     rx_s, rx_r, ry_s, ry_r, r2_s, r2_r, r3_s, r3_r, core_s, core_r,
 ):
@@ -107,6 +107,13 @@
         book_ref.at[pl.ds(pl.multiple_of(low * span, span), span)], wide, load_sem
     )
     load.start()
+    quarter = pl.ds(pl.multiple_of(dp * half, half), half)
+    adam_in = [
+        pltpu.make_async_copy(src, adam.at[n], adam_s.at[n])
+        for n, src in enumerate((book_ref.at[quarter], one_ref.at[0], two_ref.at[0]))
+    ]
+    for copy in adam_in:
+        copy.start()
 
     barrier = pltpu.get_barrier_semaphore()
     partners = (
@@ -139,17 +146,38 @@
     codes_t[...] = wide[...].T.astype(BF)
     arrive(first)
     tgt_all[x, y] = jnp.sum(tgt_z[...], axis=0)
-    second = (
-        [push(tgt_all.at[x, y], tgt_all.at[x, y], t2_s.at[k], t2_r.at[k], to_y(k)) for k in range(1, NY)]
-        + [push(rows.at[0, x, y], rows.at[0, x, y], g2_s.at[0, k], g2_r.at[0, k], to_y(k)) for k in range(1, NY)]
-        + [push(rows.at[1, x, y], rows.at[1, x, y], g2_s.at[1, k], g2_r.at[1, k], to_x(k)) for k in range(1, NX)]
-    )
-    arrive(second)
-    third_tgt = [push(tgt_all.at[x], tgt_all.at[x], t3_s.at[k], t3_r.at[k], to_x(k)) for k in range(1, NX)]
-    third_lat, third_up = {}, {}
-    for k in (1, NX - 1, 2) if NX > 2 else (1,):
-        third_lat[k] = push(rows.at[0, x], rows.at[0, x], g3_s.at[0, k], g3_r.at[0, k], to_x(k))
-        third_up[k] = push(rows.at[1, :, y], rows.at[1, :, y], g3_s.at[1, k], g3_r.at[1, k], to_y(k))
+    tgt_two = [push(tgt_all.at[x, y], tgt_all.at[x, y], t2_s.at[k], t2_r.at[k], to_y(k)) for k in range(1, NY)]
+    near_x = [1, NX - 1, 2] if NX > 2 else [1]
+    near_y = [1, NY - 1, 2] if NY > 2 else [1]
+
+    def lat_to_x(j, k):
+        part = rows.at[0, x, at_y(j)]
+        return push(part, part, gx_s.at[0, j, k], gx_r.at[0, j, k], to_x(k))
+
+    def up_to_y(j, k):
+        part = rows.at[1, at_x(j), y]
+        return push(part, part, gx_s.at[1, j, k], gx_r.at[1, j, k], to_y(k))
+
+    lat_two, up_two, lat_three, up_three = {}, {}, {}, {}
+    for k in near_y:
+        lat_two[k] = push(rows.at[0, x, y], rows.at[0, x, y], g2_s.at[0, k], g2_r.at[0, k], to_y(k))
+    for k in near_x:
+        up_two[k] = push(rows.at[1, x, y], rows.at[1, x, y], g2_s.at[1, k], g2_r.at[1, k], to_x(k))
+    for k in near_x:
+        lat_three[0, k] = lat_to_x(0, k)
+    for k in near_y:
+        up_three[0, k] = up_to_y(0, k)
+    arrive(tgt_two)
+    tgt_three = [push(tgt_all.at[x], tgt_all.at[x], t3_s.at[k], t3_r.at[k], to_x(k)) for k in range(1, NX)]
+    for n in range(max(len(near_x), len(near_y))):
+        if n < len(near_y):
+            arrive([lat_two[near_y[n]]])
+            for k in near_x:
+                lat_three[NY - near_y[n], k] = lat_to_x(NY - near_y[n], k)
+        if n < len(near_x):
+            arrive([up_two[near_x[n]]])
+            for k in near_y:
+                up_three[NX - near_x[n], k] = up_to_y(NX - near_x[n], k)
 
     pairs = NY // 2
 
@@ -161,46 +189,46 @@
 
     pieces = span // chunk
 
-    def scores(px):
-        def body(j, carry):
-            py = j * 2
-            g = px * NY + py
-            lat_b = row_block(0, px, py)
-            peak = jnp.full((16, 2 * width), -jnp.inf, F32)
-            for c in range(pieces):
-                s = rows_dot(codes[piece(c)], lat_b)
-                expo[g, piece(c)] = s[:, :width]
-                expo[g + 1, piece(c)] = s[:, width:]
-                peak = jnp.maximum(peak, fold_rows(s, jnp.max))
-            peak = jnp.max(peak, axis=0, keepdims=True)
-            stat_own[px, 0, py] = peak[:, :width]
-            stat_own[px, 0, py + 1] = peak[:, width:]
-            return carry
-
-        lax.fori_loop(0, pairs, body, 0)
-
-    def sums(b, carry):
-        px, py = lax.div(b, pairs), lax.rem(b, pairs) * 2
-        up_b = row_block(1, px, py)
-        shift = jnp.concatenate([stat_own[px, 0, py], stat_own[px, 0, py + 1]], axis=1) * SCALE
+    def pair_rows(part, pair):
+        return jnp.concatenate(
+            [rows[part, px, py].reshape(width, channels) for px, py in pair], axis=0
+        )
+
+    def scores(pair):
+        (g, px, py), (h, qx, qy) = [(cx * NY + cy, cx, cy) for cx, cy in pair]
+        lat_b = pair_rows(0, pair)
+        peak = jnp.full((16, 2 * width), -jnp.inf, F32)
+        for c in range(pieces):
+            s = rows_dot(codes[piece(c)], lat_b)
+            expo[g, piece(c)] = s[:, :width]
+            expo[h, piece(c)] = s[:, width:]
+            peak = jnp.maximum(peak, fold_rows(s, jnp.max))
+        peak = jnp.max(peak, axis=0, keepdims=True)
+        stat_own[px, 0, py] = peak[:, :width]
+        stat_own[qx, 0, qy] = peak[:, width:]
+        return peak
+
+    def sums(pair, peak):
+        (g, px, py), (h, qx, qy) = [(cx * NY + cy, cx, cy) for cx, cy in pair]
+        up_b = pair_rows(1, pair)
+        shift = peak * SCALE
         mass = jnp.zeros((16, 2 * width), F32)
         weighted = jnp.zeros((16, 2 * width), F32)
         for c in range(pieces):
             a = rows_dot(codes[piece(c)], up_b)
-            s = jnp.concatenate([expo[2 * b, piece(c)], expo[2 * b + 1, piece(c)]], axis=1)
+            s = jnp.concatenate([expo[g, piece(c)], expo[h, piece(c)]], axis=1)
             e = jnp.exp2(s * SCALE - shift)
-            expo[2 * b, piece(c)] = e[:, :width]
-            expo[2 * b + 1, piece(c)] = e[:, width:]
-            aff[2 * b, piece(c)] = a[:, :width]
-            aff[2 * b + 1, piece(c)] = a[:, width:]
+            expo[g, piece(c)] = e[:, :width]
+            expo[h, piece(c)] = e[:, width:]
+            aff[g, piece(c)] = a[:, :width]
+            aff[h, piece(c)] = a[:, width:]
             mass = mass + fold_rows(e, jnp.sum)
             weighted = weighted + fold_rows(e * a, jnp.sum)
         mass = jnp.sum(mass, axis=0, keepdims=True)
         weighted = jnp.sum(weighted, axis=0, keepdims=True)
         for k, value in enumerate((mass, weighted)):
             stat_own[px, k + 1, py] = value[:, :width]
-            stat_own[px, k + 1, py + 1] = value[:, width:]
-        return carry
+            stat_own[qx, k + 1, qy] = value[:, width:]
 
     def back_rows(out, px, py):
         g = px * NY + py
@@ -230,6 +258,7 @@
         back_rows(quant_out, px, py)
         return carry
 
+    far_plane = (2, 1, 3, 0) if NX > 2 else (1, 0)
     side_c = channels // 2
     lower, upper = pl.ds(0, side_c), pl.ds(side_c, side_c)
 
@@ -284,17 +313,29 @@
             total = total + rs_three[n, at_z(k)].astype(F32)
         return total
 
-    arrive(third_tgt)
-    lax.fori_loop(0, blocks, one_hot, 0)
-    scores(x)
-    for k in third_lat:
-        arrive([third_lat[k]])
-        scores(at_x(NX - k))
-    arrive(third_up.values())
-    quant_one = []
-    for k in (2, 1, 3, 0) if NX > 2 else (1, 0):
-        quant_one += send_plane(1, quant_out, k)
-    lax.fori_loop(0, blocks, sums, 0)
+    def late(cell):
+        rank = [k if k < 2 else NX - k + (NX if k == 2 else 0) for k in cell]
+        return (min(cell) > 0) * max(rank), sum(rank)
+
+    cells = sorted([(i, j) for i in range(NX) for j in range(NY)], key=late)
+    here = set()
+
+    def arrive_once(copy):
+        if id(copy) not in here:
+            here.add(id(copy))
+            arrive([copy])
+
+    for n in range(0, groups, 2):
+        pair = [(at_x(i), at_y(j)) for i, j in cells[n : n + 2]]
+        for i, j in cells[n : n + 2]:
+            if i:
+                arrive_once(lat_three[j, NX - i])
+        peak = scores(pair)
+        for i, j in cells[n : n + 2]:
+            if j:
+                arrive_once(up_three[i, NY - j])
+        sums(pair, peak)
+    arrive(tgt_three)
 
     sx = [push(stat_own.at[at_x(k)], stat_x.at[x], sx_s.at[k], sx_r.at[k], to_x(k)) for k in range(1, NX)]
 
@@ -303,26 +344,28 @@
         wide[pl.ds(pl.multiple_of(at, chunk), chunk)] = back_codes(1, at)
         return carry
 
-    lax.fori_loop(0, pieces, picked, 0)
+    early = blocks * 5 // 8
+    lax.fori_loop(0, early, one_hot, 0)
     arrive(sx)
     merged = merge_stats([stat_own[x]] + [stat_x[at_x(k)] for k in range(1, NX)])
     for k in range(3):
         stat_mid[0, k] = merged[k]
     sy = [push(stat_mid.at[0], stat_y.at[y], sy_s.at[k], sy_r.at[k], to_y(k)) for k in range(1, NY)]
-    arrive(quant_one)
-    quant_two = reduce_one(1, quant_out)
+    lax.fori_loop(early, blocks, one_hot, 0)
     arrive(sy)
     merged = merge_stats([merged] + [stat_y[at_y(k)] for k in range(1, NY)])
     for k in range(3):
         stat_mid[1, k] = merged[k]
     sz = [push(stat_mid.at[1], stat_z.at[z], sz_s.at[k], sz_r.at[k], to_z(k)) for k in far_first]
-    arrive(quant_two)
-    quant_three = reduce_two(1)
+    quant_one = []
+    for k in far_plane:
+        quant_one += send_plane(1, quant_out, k)
+    lax.fori_loop(0, pieces, picked, 0)
     arrive(sz)
     peak, mass, weighted = merge_stats([merged] + [stat_z[at_z(k)] for k in range(1, NZ)])
     for k, value in enumerate((peak, logit_scale / mass, weighted / mass)):
         stat_fin[x, k] = value
-    arrive([push(stat_fin.at[x], stat_fin.at[x], sf_s.at[k], sf_r.at[k], to_x(k)) for k in range(1, NX)])
+    sf = [push(stat_fin.at[x], stat_fin.at[x], sf_s.at[k], sf_r.at[k], to_x(k)) for k in range(1, NX)]
 
     def weigh(px):
         def body(j, carry):
@@ -342,10 +385,14 @@
 
         lax.fori_loop(0, pairs, body, 0)
 
-    soft_one = []
-    for k in (2, 1, 3, 0) if NX > 2 else (1, 0):
+    weigh(x)
+    arrive(sf)
+    soft_one = send_plane(0, soft_out, 0)
+    for k in far_plane[:-1]:
         weigh(at_x(k))
         soft_one += send_plane(0, soft_out, k)
+    arrive(quant_one)
+    quant_two = reduce_one(1, quant_out)
 
     def grad_other(c, carry):
         at = (1 - core) * half + c * chunk
@@ -361,14 +408,31 @@
     def grad_own(c, carry):
         at = core * half + c * chunk
         where = pl.ds(pl.multiple_of(at, chunk), chunk)
-        code_ref[pl.ds(pl.multiple_of(c * chunk, chunk), chunk)] = back_codes(0, at) + wide[where]
+        own_grad[pl.ds(pl.multiple_of(c * chunk, chunk), chunk)] = back_codes(0, at) + wide[where]
         return carry
 
     lax.fori_loop(0, half // chunk, grad_own, 0)
+    arrive(quant_two)
+    quant_three = reduce_two(1)
     arrive(soft_two)
     soft_three = reduce_two(0)
+    for copy in adam_in:
+        copy.wait()
     swap.wait_recv()
-    code_ref[...] = code_ref[...] + code_in[...].astype(F32)
+
+    def update(c, carry):
+        where = pl.ds(pl.multiple_of(c * chunk, chunk), chunk)
+        slope = own_grad[where] + code_in[where].astype(F32)
+        fresh_one = beta_one * adam[1, where] + (1.0 - beta_one) * slope
+        fresh_two = beta_two * adam[2, where] + (1.0 - beta_two) * slope * slope
+        adam[1, where] = fresh_one
+        adam[2, where] = fresh_two
+        adam[0, where] = adam[0, where] - learn_rate * (fresh_one / (1.0 - beta_one**ADAM_STEP)) / (
+            jnp.sqrt(fresh_two / (1.0 - beta_two**ADAM_STEP)) + adam_eps
+        )
+        return carry
+
+    lax.fori_loop(0, half // chunk, update, 0)
     arrive(quant_three)
     terms_ref[1] = reduce_three(1)
     arrive(soft_three)
@@ -377,7 +441,7 @@
         copy.wait_send()
 
 
-def exchange(latents, upstream, targets, codebook):
+def exchange(latents, upstream, targets, codebook, moment_one, moment_two):
     own_rows, channels = latents.shape
     width = own_rows * NZ
     span = codebook.shape[0] // 2
@@ -387,6 +451,7 @@
     dma = pltpu.SemaphoreType.DMA
     side_c = channels // 2
     in_vmem = pl.BlockSpec(memory_space=pltpu.VMEM)
+    anywhere = pl.BlockSpec(memory_space=pl.ANY)
     scratch = [
         pltpu.VMEM((2, NX, NY, NZ, own_rows, channels), BF),
         pltpu.VMEM((NZ, 1, width), jnp.int32),
@@ -412,8 +477,9 @@
         pltpu.VMEM((NX, 3, NY, 1, width), F32),
         pltpu.VMEM((half, channels), BF),
         pltpu.VMEM((half, channels), BF),
-        dma,
-        dma((NZ,)), dma((NZ,)), dma((2, NX)), dma((2, NX)), dma((2, NX)), dma((2, NX)),
+        pltpu.VMEM((half, channels), F32),
+        dma, dma((3,)),
+        dma((NZ,)), dma((NZ,)), dma((2, NX)), dma((2, NX)), dma((2, NX, NX)), dma((2, NX, NX)),
         dma((NZ,)), dma((NZ,)), dma((NY,)), dma((NY,)), dma((NX,)), dma((NX,)),
         dma((NX,)), dma((NX,)), dma((NY,)), dma((NY,)), dma((NZ,)), dma((NZ,)), dma((NX,)), dma((NX,)),
         dma((2, NX)), dma((2, NX)), dma((2, NX, NY)), dma((2, NX, NY)),
@@ -423,65 +489,34 @@
     return pl.pallas_call(
         functools.partial(kernel, chunk),
         out_shape=(
-            jax.ShapeDtypeStruct((2, own_rows, channels), F32),
-            jax.ShapeDtypeStruct((half, channels), F32),
+            pltpu.VMEM((2, own_rows, channels), F32),
+            pltpu.VMEM((3, half, channels), F32),
         ),
-        in_specs=[in_vmem, in_vmem, pl.BlockSpec(memory_space=pltpu.SMEM), pl.BlockSpec(memory_space=pl.ANY)],
+        in_specs=[in_vmem, in_vmem, pl.BlockSpec(memory_space=pltpu.SMEM), anywhere, anywhere, anywhere],
         out_specs=(in_vmem, in_vmem),
         scratch_shapes=scratch,
         compiler_params=pltpu.CompilerParams(
-            collective_id=0, has_side_effects=True, vmem_limit_bytes=60 * 1024 * 1024
+            collective_id=0, has_side_effects=True, vmem_limit_bytes=57 * 1024 * 1024
         ),
-    )(latents, upstream, targets, codebook)
-
-
-def finish(terms, lat, grad, book, one, two, quant_ref, lat_ref, book_ref, one_ref, two_ref, held, sem_in, sem_out):
-    quarter = grad.shape[0]
-    steps = 4
-    size = quarter // steps
-    own = lax.axis_index("dp") * quarter
-    sources = (grad, book, one.at[0], two.at[0])
-    targets = (book_ref.at[0], one_ref.at[0], two_ref.at[0])
-    fix_one = 1.0 - beta_one**ADAM_STEP
-    fix_two = 1.0 - beta_two**ADAM_STEP
-
-    def fetch(n, c):
-        start = own + c * size if n == 1 else c * size
-        where = pl.ds(pl.multiple_of(start, size), size)
-        return pltpu.make_async_copy(sources[n].at[where], held.at[n, pl.ds(c * size, size)], sem_in.at[n, c])
-
-    def put(n, c):
-        where = pl.ds(c * size, size)
-        return pltpu.make_async_copy(held.at[4 + n, where], targets[n].at[where], sem_out.at[n, c])
-
-    for c in range(steps):
-        for n in range(4):
-            fetch(n, c).start()
+    )(latents, upstream, targets, codebook, moment_one, moment_two)
+
+
+def finish(terms, lat, fresh, quant_ref, lat_ref, book_ref, one_ref, two_ref, sems):
+    copies = [
+        pltpu.make_async_copy(fresh.at[n], target.at[0], sems.at[n])
+        for n, target in enumerate((book_ref, one_ref, two_ref))
+    ]
+    for copy in copies:
+        copy.start()
     quant = terms[1]
     quant_ref[...] = quant.astype(BF)
     lat_ref[...] = terms[0] + commit_weight * (lat[...].astype(F32) - quant)
-    for c in range(steps):
-        for n in range(4):
-            fetch(n, c).wait()
-        where = pl.ds(c * size, size)
-        slope = held[0, where]
-        fresh_one = beta_one * held[2, where] + (1.0 - beta_one) * slope
-        fresh_two = beta_two * held[3, where] + (1.0 - beta_two) * slope * slope
-        held[5, where] = fresh_one
-        held[6, where] = fresh_two
-        held[4, where] = held[1, where] - learn_rate * (fresh_one / fix_one) / (
-            jnp.sqrt(fresh_two / fix_two) + adam_eps
-        )
-        for n in range(3):
-            put(n, c).start()
-    for c in range(steps):
-        for n in range(3):
-            put(n, c).wait()
+    for copy in copies:
+        copy.wait()
 
 
 def per_device(latents, upstream, targets, codebook, moment_one, moment_two):
-    terms, code_grad = exchange(latents, upstream, targets, codebook)
-    quarter, channels = code_grad.shape
+    terms, fresh = exchange(latents, upstream, targets, codebook, moment_one, moment_two)
     in_vmem = pl.BlockSpec(memory_space=pltpu.VMEM)
     anywhere = pl.BlockSpec(memory_space=pl.ANY)
     moment = jax.ShapeDtypeStruct(moment_one.shape, F32)
@@ -492,15 +527,11 @@
             jax.ShapeDtypeStruct(latents.shape, F32),
             moment, moment, moment,
         ),
-        in_specs=[in_vmem, in_vmem, anywhere, anywhere, anywhere, anywhere],
+        in_specs=[in_vmem, in_vmem, in_vmem],
         out_specs=(in_vmem, in_vmem, anywhere, anywhere, anywhere),
-        scratch_shapes=[
-            pltpu.VMEM((7, quarter, channels), F32),
-            pltpu.SemaphoreType.DMA((4, 4)),
-            pltpu.SemaphoreType.DMA((3, 4)),
-        ],
-        compiler_params=pltpu.CompilerParams(vmem_limit_bytes=60 * 1024 * 1024),
-    )(terms, latents, code_grad, codebook, moment_one, moment_two)
+        scratch_shapes=[pltpu.SemaphoreType.DMA((3,))],
+        compiler_params=pltpu.CompilerParams(vmem_limit_bytes=8 * 1024 * 1024),
+    )(terms, latents, fresh)
 
 
 def solution(mesh):

time: 82.9 us -> 75.8 us (0.914)
  Pallas kernels: 81.9 us -> 74.8 us
    pallas_call x1, Pallas kernels: 77.1 us -> 72.6 us  [exchange(): pl.pallas_call(functools.partial(kernel, chunk), out_shape=(pltpu.VMEM((2...]
    pallas_call x1, Pallas kernels: 4.88 us -> 2.3 us  [per_device(): pl.pallas_call(finish, out_shape=(jax.ShapeDtypeStruct(latents.shape, BF)...]
where the time goes in v3:
time: 75.8 us; the launch traced here: 75.7 us
  Pallas kernels  74.8 us (99%)
  between operations  0.82 us (1%)
    pallas_call x1, Pallas kernels, exchange(): pl.pallas_call(functools.partial(kernel, chunk), out_shape=(pltpu.VMEM((2...  72.6 us
    pallas_call x1, Pallas kernels, per_device(): pl.pallas_call(finish, out_shape=(jax.ShapeDtypeStruct(latents.shape, BF)...  2.3 us

profile of v3, /device:TPU:2, one launch (start us, length us, event | category | flops | bytes accessed | tf_op | source)
XLA Modules:
  0.0 75.7 jit_solution(9669767687486119356)
XLA Ops:
  0.6 0.0 copy-start
  0.6 72.6 %shard_map.101 = (f32[2,16,256]{2,1,0:T(8,128)S(1)}, f32[3,1024,256]{2,1,0:T(8,128)S(1)}) custom-call(bf16[16,256]{1,0:T(8,128)(2,1)} %lat.1, bf16[16,256]{1,0:T(8,128)(2,1)} %up_ref.1, s32[16]{0:T(128)} %tgt_ref.1, f32[4096,256]{1,0:T(8,128)} %book_ref.1, f32[1,1024,256]{2,1,0:T(8,128)} %one_ref.1, f32[1,1024,256]{2,1,0:T(8,128)} %two_ref.1), custom_call_target="tpu_custom_call" | custom-call | tf_op jit(solution)/shard_map/pallas_call | solution.py:489
  73.2 0.0 copy-done
  73.2 2.3 %shard_map.102 = (bf16[16,256]{1,0:T(8,128)(2,1)}, f32[16,256]{1,0:T(8,128)}, f32[1,1024,256]{2,1,0:T(8,128)}, f32[1,1024,256]{2,1,0:T(8,128)}, f32[1,1024,256]{2,1,0:T(8,128)}) custom-call(f32[2,16,256]{2,1,0:T(8,128)S(1)} %get-tuple-element.7.terms, bf16[16,256]{1,0:T(8,128)(2,1)S(1)} %copy-done, f32[3,1024,256]{2,1,0:T(8,128)S(1)} %get-tuple-element.8.fresh), custom_call_target="tpu_custom_call" | custom-call | tf_op jit(solution)/shard_map/pallas_call | solution.py:523
Async XLA Ops:
  0.6 72.6 %copy-start = (bf16[16,256]{1,0:T(8,128)(2,1)S(1)}, bf16[16,256]{1,0:T(8,128)(2,1)}, u32[]{:S(2)}) copy-start(bf16[16,256]{1,0:T(8,128)(2,1)} %lat.1) | copy-start | bytes 24580

commit v4 on v3

--- a/solution.py
+++ b/solution.py
@@ -7,7 +7,7 @@
 from jax.experimental.pallas import tpu as pltpu
 from jax.sharding import PartitionSpec as P
 
-ADAM_STEP = 100
+ADAM_2 = 100
 logit_scale = 4.0
 commit_weight = 0.5
 learn_rate = 0.001
@@ -194,41 +194,41 @@
             [rows[part, px, py].reshape(width, channels) for px, py in pair], axis=0
         )
 
-    def scores(pair):
-        (g, px, py), (h, qx, qy) = [(cx * NY + cy, cx, cy) for cx, cy in pair]
-        lat_b = pair_rows(0, pair)
-        peak = jnp.full((16, 2 * width), -jnp.inf, F32)
+    def group(cell):
+        return cell[0] * NY + cell[1]
+
+    def local_stats(pair, peak, ahead):
+        if ahead:
+            lat_n = pair_rows(0, ahead)
+            peak_n = jnp.full((16, 2 * width), -jnp.inf, F32)
+        if pair:
+            g, h = group(pair[0]), group(pair[1])
+            up_b = pair_rows(1, pair)
+            lat_b = pair_rows(0, pair)
+            shift = peak * SCALE
+            mass = jnp.zeros((16, 2 * width), F32)
+            weighted = jnp.zeros((16, 2 * width), F32)
         for c in range(pieces):
-            s = rows_dot(codes[piece(c)], lat_b)
-            expo[g, piece(c)] = s[:, :width]
-            expo[h, piece(c)] = s[:, width:]
-            peak = jnp.maximum(peak, fold_rows(s, jnp.max))
-        peak = jnp.max(peak, axis=0, keepdims=True)
-        stat_own[px, 0, py] = peak[:, :width]
-        stat_own[qx, 0, qy] = peak[:, width:]
-        return peak
-
-    def sums(pair, peak):
-        (g, px, py), (h, qx, qy) = [(cx * NY + cy, cx, cy) for cx, cy in pair]
-        up_b = pair_rows(1, pair)
-        shift = peak * SCALE
-        mass = jnp.zeros((16, 2 * width), F32)
-        weighted = jnp.zeros((16, 2 * width), F32)
-        for c in range(pieces):
-            a = rows_dot(codes[piece(c)], up_b)
-            s = jnp.concatenate([expo[g, piece(c)], expo[h, piece(c)]], axis=1)
-            e = jnp.exp2(s * SCALE - shift)
-            expo[g, piece(c)] = e[:, :width]
-            expo[h, piece(c)] = e[:, width:]
-            aff[g, piece(c)] = a[:, :width]
-            aff[h, piece(c)] = a[:, width:]
-            mass = mass + fold_rows(e, jnp.sum)
-            weighted = weighted + fold_rows(e * a, jnp.sum)
-        mass = jnp.sum(mass, axis=0, keepdims=True)
-        weighted = jnp.sum(weighted, axis=0, keepdims=True)
-        for k, value in enumerate((mass, weighted)):
-            stat_own[px, k + 1, py] = value[:, :width]
-            stat_own[qx, k + 1, qy] = value[:, width:]
+            if ahead:
+                s = rows_dot(codes[piece(c)], lat_n)
+                peak_n = jnp.maximum(peak_n, fold_rows(s, jnp.max))
+            if pair:
+                a = rows_dot(codes[piece(c)], up_b)
+                s = rows_dot(codes[piece(c)], lat_b)
+                e = jnp.exp2(s * SCALE - shift)
+                expo[g, piece(c)] = e[:, :width]
+                expo[h, piece(c)] = e[:, width:]
+                aff[g, piece(c)] = a[:, :width]
+                aff[h, piece(c)] = a[:, width:]
+                mass = mass + fold_rows(e, jnp.sum)
+                weighted = weighted + fold_rows(e * a, jnp.sum)
+        if pair:
+            mass = jnp.sum(mass, axis=0, keepdims=True)
+            weighted = jnp.sum(weighted, axis=0, keepdims=True)
+            for k, value in enumerate((peak, mass, weighted)):
+                for n, (px, py) in enumerate(pair):
+                    stat_own[px, k, py] = value[:, n * width : (n + 1) * width]
+        return jnp.max(peak_n, axis=0, keepdims=True) if ahead else None
 
     def back_rows(out, px, py):
         g = px * NY + py
@@ -325,16 +325,17 @@
             here.add(id(copy))
             arrive([copy])
 
-    for n in range(0, groups, 2):
-        pair = [(at_x(i), at_y(j)) for i, j in cells[n : n + 2]]
+    pair, peak = None, None
+    for n in range(0, groups + 2, 2):
         for i, j in cells[n : n + 2]:
             if i:
                 arrive_once(lat_three[j, NX - i])
-        peak = scores(pair)
-        for i, j in cells[n : n + 2]:
+        for i, j in cells[n - 2 : n] if n else ():
             if j:
                 arrive_once(up_three[i, NY - j])
-        sums(pair, peak)
+        ahead = [(at_x(i), at_y(j)) for i, j in cells[n : n + 2]]
+        peak = local_stats(pair, peak, ahead)
+        pair = ahead
     arrive(tgt_three)
 
     sx = [push(stat_own.at[at_x(k)], stat_x.at[x], sx_s.at[k], sx_r.at[k], to_x(k)) for k in range(1, NX)]
@@ -371,16 +372,28 @@
         def body(j, carry):
             py = j * 2
             g = px * NY + py
+            fade, mean = [], []
             for side in range(2):
-                fade = (
+                fade.append(
                     jnp.exp2((stat_own[px, 0, py + side] - stat_fin[px, 0, py + side]) * SCALE)
                     * stat_fin[px, 1, py + side]
                 )
-                mean = stat_fin[px, 2, py + side]
-                for c in range(pieces):
-                    w = expo[g + side, piece(c)] * fade * (aff[g + side, piece(c)] - mean)
-                    weights[g + side, piece(c)] = w.astype(BF)
-            back_rows(soft_out, px, py)
+                mean.append(stat_fin[px, 2, py + side])
+            total = None
+            for c in range(0, pieces, 2):
+                pair = []
+                for side in range(2):
+                    parts = []
+                    for d in range(c, c + 2):
+                        w = expo[g + side, piece(d)] * fade[side] * (aff[g + side, piece(d)] - mean[side])
+                        weights[g + side, piece(d)] = w.astype(BF)
+                        parts.append(w.astype(BF))
+                    pair.append(jnp.concatenate(parts, axis=0))
+                term = plain_dot(codes_t[:, c * chunk : (c + 2) * chunk], jnp.concatenate(pair, axis=1))
+                total = term if total is None else total + term
+            total = total.astype(BF)
+            soft_out[px, py] = total[:, :width]
+            soft_out[px, py + 1] = total[:, width:]
             return carry
 
         lax.fori_loop(0, pairs, body, 0)
@@ -427,8 +440,8 @@
         fresh_two = beta_two * adam[2, where] + (1.0 - beta_two) * slope * slope
         adam[1, where] = fresh_one
         adam[2, where] = fresh_two
-        adam[0, where] = adam[0, where] - learn_rate * (fresh_one / (1.0 - beta_one**ADAM_STEP)) / (
-            jnp.sqrt(fresh_two / (1.0 - beta_two**ADAM_STEP)) + adam_eps
+        adam[0, where] = adam[0, where] - learn_rate * (fresh_one / (1.0 - beta_one**ADAM_2)) / (
+            jnp.sqrt(fresh_two / (1.0 - beta_two**ADAM_2)) + adam_eps
         )
         return carry
 

time: 75.8 us -> 74.5 us (0.983)
  Pallas kernels: 74.8 us -> 73.6 us
    pallas_call x1, Pallas kernels: 72.6 us -> 71.3 us  [exchange(): pl.pallas_call(functools.partial(kernel, chunk), out_shape=(pltpu.VMEM((2...]
where the time goes in v4:
time: 74.5 us; the launch traced here: 74.4 us
  Pallas kernels  73.6 us (99%)
  between operations  0.82 us (1%)
    pallas_call x1, Pallas kernels, exchange(): pl.pallas_call(functools.partial(kernel, chunk), out_shape=(pltpu.VMEM((2...  71.3 us
    pallas_call x1, Pallas kernels, per_device(): pl.pallas_call(finish, out_shape=(jax.ShapeDtypeStruct(latents.shape, BF)...  2.3 us

profile of v4, /device:TPU:2, one launch (start us, length us, event | category | flops | bytes accessed | tf_op | source)
XLA Modules:
  0.0 74.4 jit_solution(4917735803177436107)
XLA Ops:
  0.6 0.0 copy-start
  0.6 71.3 %shard_map.101 = (f32[2,16,256]{2,1,0:T(8,128)S(1)}, f32[3,1024,256]{2,1,0:T(8,128)S(1)}) custom-call(bf16[16,256]{1,0:T(8,128)(2,1)} %lat.1, bf16[16,256]{1,0:T(8,128)(2,1)} %up_ref.1, s32[16]{0:T(128)} %tgt_ref.1, f32[4096,256]{1,0:T(8,128)} %book_ref.1, f32[1,1024,256]{2,1,0:T(8,128)} %one_ref.1, f32[1,1024,256]{2,1,0:T(8,128)} %two_ref.1), custom_call_target="tpu_custom_call" | custom-call | tf_op jit(solution)/shard_map/pallas_call | solution.py:502
  71.9 0.0 copy-done
  71.9 2.3 %shard_map.102 = (bf16[16,256]{1,0:T(8,128)(2,1)}, f32[16,256]{1,0:T(8,128)}, f32[1,1024,256]{2,1,0:T(8,128)}, f32[1,1024,256]{2,1,0:T(8,128)}, f32[1,1024,256]{2,1,0:T(8,128)}) custom-call(f32[2,16,256]{2,1,0:T(8,128)S(1)} %get-tuple-element.7.terms, bf16[16,256]{1,0:T(8,128)(2,1)S(1)} %copy-done, f32[3,1024,256]{2,1,0:T(8,128)S(1)} %get-tuple-element.8.fresh), custom_call_target="tpu_custom_call" | custom-call | tf_op jit(solution)/shard_map/pallas_call | solution.py:536
Async XLA Ops:
  0.6 71.3 %copy-start = (bf16[16,256]{1,0:T(8,128)(2,1)S(1)}, bf16[16,256]{1,0:T(8,128)(2,1)}, u32[]{:S(2)}) copy-start(bf16[16,256]{1,0:T(8,128)(2,1)} %lat.1) | copy-start | bytes 24580

commit v5 on v4

--- a/solution.py
+++ b/solution.py
@@ -515,8 +515,12 @@
 
 
 def finish(terms, lat, fresh, quant_ref, lat_ref, book_ref, one_ref, two_ref, sems):
+    size = fresh.shape[1] // 4
     copies = [
-        pltpu.make_async_copy(fresh.at[n], target.at[0], sems.at[n])
+        pltpu.make_async_copy(
+            fresh.at[n, pl.ds(c * size, size)], target.at[0, pl.ds(c * size, size)], sems.at[n, c]
+        )
+        for c in range(4)
         for n, target in enumerate((book_ref, one_ref, two_ref))
     ]
     for copy in copies:
@@ -542,7 +546,7 @@
         ),
         in_specs=[in_vmem, in_vmem, in_vmem],
         out_specs=(in_vmem, in_vmem, anywhere, anywhere, anywhere),
-        scratch_shapes=[pltpu.SemaphoreType.DMA((3,))],
+        scratch_shapes=[pltpu.SemaphoreType.DMA((3, 4))],
         compiler_params=pltpu.CompilerParams(vmem_limit_bytes=8 * 1024 * 1024),
     )(terms, latents, fresh)
 

time: 74.5 us -> 74.6 us (level)
  no operation moved by 1% of the time
where the time goes in v5:
time: 74.6 us; the launch traced here: 74.4 us
  Pallas kernels  73.6 us (99%)
  between operations  0.82 us (1%)
    pallas_call x1, Pallas kernels, exchange(): pl.pallas_call(functools.partial(kernel, chunk), out_shape=(pltpu.VMEM((2...  71.3 us
    pallas_call x1, Pallas kernels, per_device(): pl.pallas_call(finish, out_shape=(jax.ShapeDtypeStruct(latents.shape, BF)...  2.36 us

profile of v5, /device:TPU:2, one launch (start us, length us, event | category | flops | bytes accessed | tf_op | source)
XLA Modules:
  0.0 74.4 jit_solution(5798463449364344773)
XLA Ops:
  0.6 0.0 copy-start
  0.6 71.3 %shard_map.101 = (f32[2,16,256]{2,1,0:T(8,128)S(1)}, f32[3,1024,256]{2,1,0:T(8,128)S(1)}) custom-call(bf16[16,256]{1,0:T(8,128)(2,1)} %lat.1, bf16[16,256]{1,0:T(8,128)(2,1)} %up_ref.1, s32[16]{0:T(128)} %tgt_ref.1, f32[4096,256]{1,0:T(8,128)} %book_ref.1, f32[1,1024,256]{2,1,0:T(8,128)} %one_ref.1, f32[1,1024,256]{2,1,0:T(8,128)} %two_ref.1), custom_call_target="tpu_custom_call" | custom-call | tf_op jit(solution)/shard_map/pallas_call | solution.py:502
  71.9 0.0 copy-done
  71.9 2.4 %shard_map.102 = (bf16[16,256]{1,0:T(8,128)(2,1)}, f32[16,256]{1,0:T(8,128)}, f32[1,1024,256]{2,1,0:T(8,128)}, f32[1,1024,256]{2,1,0:T(8,128)}, f32[1,1024,256]{2,1,0:T(8,128)}) custom-call(f32[2,16,256]{2,1,0:T(8,128)S(1)} %get-tuple-element.7.terms, bf16[16,256]{1,0:T(8,128)(2,1)S(1)} %copy-done, f32[3,1024,256]{2,1,0:T(8,128)S(1)} %get-tuple-element.8.fresh), custom_call_target="tpu_custom_call" | custom-call | tf_op jit(solution)/shard_map/pallas_call | solution.py:540
Async XLA Ops:
  0.6 71.3 %copy-start = (bf16[16,256]{1,0:T(8,128)(2,1)S(1)}, bf16[16,256]{1,0:T(8,128)(2,1)}, u32[]{:S(2)}) copy-start(bf16[16,256]{1,0:T(8,128)(2,1)} %lat.1) | copy-start | bytes 24580
